TPU v7x, 32 devices: a whole 2x2x4 slice. The times are simulated.
32 devices in a mesh: ctx: 8 (over y, x, core), wsh: 4 (over z).
Axes of the slice: x: 2, y: 2, z: 4, core: 2. Of those that a mesh axis runs over, the one named last changes fastest.
Arguments:
- block_in: bfloat16 [4, 8192, 800], P('wsh', 'ctx'), may hold values from -6 to 6
- out_grad: bfloat16 [4, 8192, 800], P('wsh', 'ctx'), may hold values from -6 to 6
- segments: int32 [4, 8192], P('wsh', 'ctx'), may hold values from 0 to 127, as said below
- block_deal: int32 [64], replicated, may hold values from 0 to 63, as said below
- weight_in: bfloat16 [800, 400], P(None, 'wsh'), may hold values from -0.21875 to 0.21875
- weight_conv: bfloat16 [3, 400, 400], P(None, None, 'wsh'), may hold values from -0.1875 to 0.1875
- weight_out: bfloat16 [400, 800], P(None, 'wsh'), may hold values from -0.3125 to 0.3125
- gain_first: bfloat16 [800], P('wsh'), may hold values from 0.25 to 1.75
- shift_first: bfloat16 [800], P('wsh'), may hold values from -3 to 3
- gain_second: bfloat16 [400], P('wsh'), may hold values from 0.25 to 1.75
- shift_second: bfloat16 [400], P('wsh'), may hold values from -3 to 3
- gain_third: bfloat16 [400], P('wsh'), may hold values from 0.25 to 1.75
- shift_third: bfloat16 [400], P('wsh'), may hold values from -3 to 3
- bias_first: bfloat16 [400], P('wsh'), may hold values from -3 to 3
- bias_conv: bfloat16 [400], P('wsh'), may hold values from -3 to 3
- bias_out: bfloat16 [800], P('wsh'), may hold values from -3 to 3
Outputs:
- block_out: bfloat16 [4, 8192, 800], P('wsh', 'ctx')
- input_grad: float32 [4, 8192, 800], P('wsh', 'ctx')
- grad_weight_in: float32 [800, 400], P(None, 'wsh')
- grad_weight_conv: float32 [3, 400, 400], P(None, None, 'wsh')
- grad_weight_out: float32 [400, 800], P(None, 'wsh')
- grad_gain_first: float32 [800], P('wsh')
- grad_shift_first: float32 [800], P('wsh')
- grad_gain_second: float32 [400], P('wsh')
- grad_shift_second: float32 [400], P('wsh')
- grad_gain_third: float32 [400], P('wsh')
- grad_shift_third: float32 [400], P('wsh')
- grad_bias_first: float32 [400], P('wsh')
- grad_bias_conv: float32 [400], P('wsh')
- grad_bias_out: float32 [800], P('wsh')
Inputs may be any that keep to these rules, and one draw needn't show every extreme that they name: `block_deal`: A permutation of the 64 blocks of a sequence; the slots of one device along ctx come in pairs 2q, 2q + 1 that hold blocks j and 63 - j. `segments`: read in the natural order of blocks given by block_deal, the numbers of a sequence start at 0, never fall, rise by at most one from a position to the next, and end at 127; a document may cross block and device boundaries.
All inputs are finite; a program needn't handle non-finite values.
Results may differ from a plain program's by a relative error of at most 0.0066.
Values may be sent and summed in bfloat16 or wider, within the bound.
A program may use at most 256 MiB of HBM per device.

v0:
```python
import jax
import jax.numpy as jnp
from jax import lax
from jax.sharding import PartitionSpec as P

KERNEL_TAPS = 3
DILATION_STEP = 16
BLK = 128


EPS = 1e-05


def norm_ahead(values, gain, shift):
    centre = jnp.mean(values, -1, keepdims=True)
    centred = values - centre
    scaled = lax.rsqrt(jnp.mean(centred * centred, -1, keepdims=True) + EPS)
    normed = centred * scaled
    return (normed, scaled, normed * gain + shift)


def norm_behind(upstream, normed, scaled, gain):
    grad_normed = upstream * gain
    grad_gain = jnp.sum(upstream * normed, 0)
    grad_shift = jnp.sum(upstream, 0)
    first_mean = jnp.mean(grad_normed, -1, keepdims=True)
    second_mean = jnp.mean(grad_normed * normed, -1, keepdims=True)
    return (scaled * (grad_normed - first_mean - normed * second_mean), grad_gain, grad_shift)


def silu_slope(values):
    logistic = jax.nn.sigmoid(values)
    return logistic * (1.0 + values * (1.0 - logistic))


def on_device(
    block_in,
    out_grad,
    segments,
    block_deal,
    weight_in,
    weight_conv,
    weight_out,
    gain_first,
    shift_first,
    gain_second,
    shift_second,
    gain_third,
    shift_third,
    bias_first,
    bias_conv,
    bias_out,
):
    gathered = (
        lax.all_gather(weight_in, "wsh", axis=1, tiled=True),
        lax.all_gather(weight_conv, "wsh", axis=2, tiled=True),
        lax.all_gather(weight_out, "wsh", axis=1, tiled=True),
        lax.all_gather(gain_first, "wsh", axis=0, tiled=True),
        lax.all_gather(shift_first, "wsh", axis=0, tiled=True),
        lax.all_gather(gain_second, "wsh", axis=0, tiled=True),
        lax.all_gather(shift_second, "wsh", axis=0, tiled=True),
        lax.all_gather(gain_third, "wsh", axis=0, tiled=True),
        lax.all_gather(shift_third, "wsh", axis=0, tiled=True),
        lax.all_gather(bias_first, "wsh", axis=0, tiled=True),
        lax.all_gather(bias_conv, "wsh", axis=0, tiled=True),
        lax.all_gather(bias_out, "wsh", axis=0, tiled=True),
    )
    full_in = gathered[0]
    full_conv = gathered[1]
    complete_output = gathered[2]
    vectors = [member.astype(jnp.float32) for member in gathered[3:]]
    (
        gain_lead,
        shift_lead,
        gain_inner,
        shift_inner,
        gain_late,
        shift_late,
        bias_lead,
        bias_middle,
        bias_late,
    ) = vectors
    row_count = block_in.shape[1]
    inner_width = full_in.shape[1]
    per_device = row_count // BLK
    block_total = per_device * lax.axis_size("ctx")
    receptive_rows = (KERNEL_TAPS - 1) * DILATION_STEP
    device = lax.axis_index("ctx")
    own_blocks = lax.dynamic_slice_in_dim(block_deal, device * per_device, per_device)
    block_ids = jnp.arange(block_total, dtype=jnp.int32)
    slot_of = jnp.sum(
        jnp.where(block_deal[None, :] == block_ids[:, None], block_ids[None, :], 0), axis=1
    )
    has_prev = own_blocks > 0
    prev_slot = jnp.take(slot_of, jnp.maximum(own_blocks - 1, 0))
    seg_local = segments[0].reshape(per_device, BLK)
    seg_sent = seg_local[:, BLK - receptive_rows :].reshape(per_device * receptive_rows)
    seg_tails = lax.all_gather(seg_sent, "ctx", axis=0, tiled=True).reshape(
        block_total, receptive_rows
    )
    seg_extended = jnp.concatenate([jnp.take(seg_tails, prev_slot, axis=0), seg_local], axis=1)
    positions = own_blocks[:, None] * BLK + jnp.arange(BLK, dtype=jnp.int32)[None, :]
    tap_masks = []
    for kernel_tap_index in range(KERNEL_TAPS):
        tap_delay = kernel_tap_index * DILATION_STEP
        start_offset = receptive_rows - tap_delay
        matching = seg_extended[:, start_offset : start_offset + BLK] == seg_local
        tap_masks.append(jnp.logical_and(matching, positions >= tap_delay))
    inputs = block_in[0].astype(jnp.float32)
    normed_one, scaled_one, pre_one = norm_ahead(inputs, gain_lead, shift_lead)
    act_first = jax.nn.silu(pre_one).astype(jnp.bfloat16)
    hidden = jnp.dot(act_first, full_in, preferred_element_type=jnp.float32) + bias_lead
    normed_two, scaled_two, pre_two = norm_ahead(hidden, gain_inner, shift_inner)
    act_second = jax.nn.silu(pre_two).astype(jnp.bfloat16)
    act_blocks = act_second.reshape(per_device, BLK, inner_width)
    whole_seq = lax.all_gather(act_second, "ctx", axis=0, tiled=True).reshape(
        block_total, BLK, inner_width
    )
    tail_rows = jnp.take(whole_seq[:, BLK - receptive_rows :], prev_slot, axis=0)
    tail_rows = jnp.where(has_prev[:, None, None], tail_rows, jnp.zeros_like(tail_rows))
    extended = jnp.concatenate([tail_rows, act_blocks], axis=1)
    conv_sum = jnp.zeros((per_device, BLK, inner_width), jnp.float32) + bias_middle
    for kernel_tap_index in range(KERNEL_TAPS):
        start_offset = receptive_rows - kernel_tap_index * DILATION_STEP
        product = jnp.einsum(
            "jrh,hg->jrg",
            extended[:, start_offset : start_offset + BLK],
            full_conv[kernel_tap_index],
            preferred_element_type=jnp.float32,
        )
        conv_sum = conv_sum + jnp.where(tap_masks[kernel_tap_index][:, :, None], product, 0.0)
    conv_out = conv_sum.reshape(row_count, inner_width)
    normed_three, scaled_three, pre_three = norm_ahead(conv_out, gain_late, shift_late)
    act_third = jax.nn.silu(pre_three).astype(jnp.bfloat16)
    branch = jnp.dot(act_third, complete_output, preferred_element_type=jnp.float32) + bias_late
    block_out = (inputs + branch).astype(jnp.bfloat16)[None]
    upstream = out_grad[0]
    grad_weight_out = jnp.einsum(
        "rh,rd->hd", act_third, upstream, preferred_element_type=jnp.float32
    )
    grad_bias_out = jnp.sum(upstream.astype(jnp.float32), 0)
    grad_third = jnp.einsum(
        "rd,hd->rh", upstream, complete_output, preferred_element_type=jnp.float32
    )
    grad_third = grad_third * silu_slope(pre_three)
    grad_conv, grad_gain_third, grad_shift_third = norm_behind(
        grad_third, normed_three, scaled_three, gain_late
    )
    grad_conv = grad_conv.astype(jnp.bfloat16)
    grad_bias_conv = jnp.sum(grad_conv.astype(jnp.float32), 0)
    grad_blocks = grad_conv.reshape(per_device, BLK, inner_width)
    grad_extended = jnp.zeros((per_device, receptive_rows + BLK, inner_width), jnp.float32)
    tap_grads = []
    masked_grads = []
    for kernel_tap_index in range(KERNEL_TAPS):
        start_offset = receptive_rows - kernel_tap_index * DILATION_STEP
        masked_grad = jnp.where(
            tap_masks[kernel_tap_index][:, :, None], grad_blocks, jnp.zeros_like(grad_blocks)
        )
        masked_grads.append(masked_grad)
        tap_grads.append(
            jnp.einsum(
                "jrh,jrg->hg",
                extended[:, start_offset : start_offset + BLK],
                masked_grad,
                preferred_element_type=jnp.float32,
            )
        )
        back_piece = jnp.einsum(
            "jrg,hg->jrh",
            masked_grad,
            full_conv[kernel_tap_index],
            preferred_element_type=jnp.float32,
        )
        grad_extended = grad_extended.at[:, start_offset : start_offset + BLK].add(back_piece)
    grad_weight_conv = jnp.stack(tap_grads, axis=0)
    grad_local = grad_extended[:, receptive_rows:]
    grad_tail = grad_extended[:, :receptive_rows]
    placement_map = jnp.logical_and(
        prev_slot[None, :] == block_ids[:, None], has_prev[None, :]
    ).astype(jnp.float32)
    padded_tail = jnp.concatenate(
        [jnp.zeros((per_device, BLK - receptive_rows, inner_width), jnp.float32), grad_tail], axis=1
    )
    spread = jnp.einsum("sj,jrh->srh", placement_map, padded_tail, precision=lax.Precision.HIGHEST)
    returned = lax.psum_scatter(
        spread.reshape(block_total * BLK, inner_width).astype(jnp.bfloat16),
        "ctx",
        scatter_dimension=0,
        tiled=True,
    ).astype(jnp.float32)
    grad_second = grad_local + returned.reshape(per_device, BLK, inner_width)
    grad_second = grad_second.reshape(row_count, inner_width)
    grad_second = grad_second * silu_slope(pre_two)
    grad_hidden, grad_gain_second, grad_shift_second = norm_behind(
        grad_second, normed_two, scaled_two, gain_inner
    )
    grad_hidden = grad_hidden.astype(jnp.bfloat16)
    grad_bias_first = jnp.sum(grad_hidden.astype(jnp.float32), 0)
    grad_weight_in = jnp.einsum(
        "rd,rh->dh", act_first, grad_hidden, preferred_element_type=jnp.float32
    )
    grad_first = jnp.einsum("rh,dh->rd", grad_hidden, full_in, preferred_element_type=jnp.float32)
    grad_first = grad_first * silu_slope(pre_one)
    grad_inputs, grad_gain_first, grad_shift_first = norm_behind(
        grad_first, normed_one, scaled_one, gain_lead
    )
    input_grad = (upstream.astype(jnp.float32) + grad_inputs)[None]
    shards = (
        lax.psum_scatter(grad_weight_in, "wsh", scatter_dimension=1, tiled=True),
        lax.psum_scatter(grad_weight_conv, "wsh", scatter_dimension=2, tiled=True),
        lax.psum_scatter(grad_weight_out, "wsh", scatter_dimension=1, tiled=True),
        lax.psum_scatter(grad_gain_first, "wsh", scatter_dimension=0, tiled=True),
        lax.psum_scatter(grad_shift_first, "wsh", scatter_dimension=0, tiled=True),
        lax.psum_scatter(grad_gain_second, "wsh", scatter_dimension=0, tiled=True),
        lax.psum_scatter(grad_shift_second, "wsh", scatter_dimension=0, tiled=True),
        lax.psum_scatter(grad_gain_third, "wsh", scatter_dimension=0, tiled=True),
        lax.psum_scatter(grad_shift_third, "wsh", scatter_dimension=0, tiled=True),
        lax.psum_scatter(grad_bias_first, "wsh", scatter_dimension=0, tiled=True),
        lax.psum_scatter(grad_bias_conv, "wsh", scatter_dimension=0, tiled=True),
        lax.psum_scatter(grad_bias_out, "wsh", scatter_dimension=0, tiled=True),
    )
    totals = lax.psum(tuple(shards), "ctx")
    return (block_out, input_grad) + tuple(totals)


def solution(mesh):
    in_specs = (
        P("wsh", "ctx", None),
        P("wsh", "ctx", None),
        P("wsh", "ctx"),
        P(),
        P(None, "wsh"),
        P(None, None, "wsh"),
        P(None, "wsh"),
        P("wsh"),
        P("wsh"),
        P("wsh"),
        P("wsh"),
        P("wsh"),
        P("wsh"),
        P("wsh"),
        P("wsh"),
        P("wsh"),
    )
    out_specs = (
        P("wsh", "ctx", None),
        P("wsh", "ctx", None),
        P(None, "wsh"),
        P(None, None, "wsh"),
        P(None, "wsh"),
        P("wsh"),
        P("wsh"),
        P("wsh"),
        P("wsh"),
        P("wsh"),
        P("wsh"),
        P("wsh"),
        P("wsh"),
        P("wsh"),
    )
    return jax.shard_map(
        on_device, mesh=mesh, in_specs=in_specs, out_specs=out_specs, check_vma=False
    )
```

profile of v0, /device:TPU:0, one launch (start us, length us, event | category | flops | bytes accessed | tf_op | source)
XLA Modules:
  0.0 495.0 jit_solution(15779923015769861360)
XLA Ops:
  7.3 1.4 fusion.91
  10.0 0.9 dynamic-update-slice.13
  10.8 0.8 dynamic-update-slice.14
  11.7 0.8 dynamic-update-slice.12
  12.5 0.8 dynamic-update-slice.15
  13.4 0.8 dynamic-update-slice.16
  14.2 0.8 dynamic-update-slice.9
  17.6 20.5 %all-reduce.26 = (bf16[800]{0:T(1024)(128)(2,1)}, bf16[400]{0:T(512)(128)(2,1)S(1)}, bf16[400]{0:T(512)(128)(2,1)S(1)}, bf16[800]{0:T(1024)(128)(2,1)S(1)}, bf16...) all-reduce(bf16[800]{0:T(1024)(128)(2,1)S(1)} %dynamic-update-slice, ...), channel_id=1, replica_groups=mesh['ctx'=8,'wsh'=4] {'wsh'}, use_global_device_ids=true, to_apply=%add.10 | all-reduce | flops 4800 | bytes 19200
  38.1 1.7 convert_reduce_fusion.1
  40.4 16.0 %all-gather = bf16[4,100,800]{2,1,0:T(8,128)(2,1)S(1)} all-gather(bf16[1,100,800]{2,1,0:T(8,128)(2,1)S(1)} %bitcast.242), channel_id=1, replica_groups=mesh['ctx'=8,'wsh'=4] {'wsh'}, dimensions={0}, use_global_device_ids=true | all-gather | bytes 800000 | tf_op jit(solution)/shard_map/all_gather | solution.py:55
  56.4 1.2 reshape.382
  57.5 1.3 fusion.16
  58.8 1.0 fusion.92
  60.2 1.5 multiply_convert_fusion.4
  63.8 8.9 %all-gather.1 = s32[8,1,256]{2,1,0:T(1,128)S(1)} all-gather(s32[1,1,256]{2,1,0:T(1,128)S(1)} %reshape.383), channel_id=1, replica_groups=mesh['ctx'=8,'wsh'=4] {'ctx'}, dimensions={0}, use_global_device_ids=true | all-gather | bytes 9216 | tf_op jit(solution)/shard_map/all_gather | solution.py:98
  72.8 1.1 copy.94
  73.8 2.1 copy.85
  76.8 1.2 gather_fusion
  77.9 1.2 compare_and_fusion
  80.3 1.5 fusion.71
  81.7 18.9 %all_gather.54 = bf16[400,800]{0,1:T(8,128)(2,1)} all-gather(bf16[400,200]{0,1:T(8,128)(2,1)S(1)} %copy.94), channel_id=1, replica_groups=mesh['ctx'=8,'wsh'=4] {'wsh'}, dimensions={1}, use_global_device_ids=true | all-gather | bytes 800000 | tf_op jit(solution)/shard_map/all_gather | solution.py:57
  100.6 29.7 %all_gather.49 = bf16[3,400,400]{1,0,2:T(4,128)(2,1)S(1)} all-gather(bf16[3,400,100]{1,0,2:T(4,128)(2,1)} %copy.85), channel_id=1, replica_groups=mesh['ctx'=8,'wsh'=4] {'wsh'}, dimensions={2}, use_global_device_ids=true | all-gather | bytes 1200000 | tf_op jit(solution)/shard_map/all_gather | solution.py:56
  130.4 1.5 copy_bitcast_fusion.1
  131.9 2.7 fusion.90
  134.6 0.9 copy-done.8
  135.5 2.1 fusion.63
  137.6 10.7 %copy.110 = bf16[8192,400]{1,0:T(8,128)(2,1)} copy(bf16[8192,400]{0,1:T(8,128)(2,1)} %all-gather.4.cloned.1.call-done) | data formatting | bytes 13107200 | tf_op jit(solution)/shard_map/reshape | solution.py:116
  148.3 3.2 slice.131
  151.5 2.3 gather_fusion.2
  153.7 1.2 copy.89
  155.0 1.4 select_select_fusion
  156.7 0.8 fusion.64
  158.3 0.9 fusion.93
  159.5 1.8 copy-done.13
  161.4 2.0 multiply_reduce_fusion.1
  166.5 1.7 pad_maximum_fusion
  168.3 4.3 fusion.36
  172.9 2.5 select_bitcast_fusion
  176.0 2.6 scatter-add.10
  178.6 1.9 slice_add_fusion.1
  180.5 8.2 %scatter-add.11 = f32[8,160,400]{1,2,0:T(8,128)} dynamic-update-slice(f32[8,160,400]{1,2,0:T(8,128)} %scatter-add.10, f32[8,128,400]{1,2,0:T(8,128)} %slice_add_fusion.1, s32[]{:T(128)} %constant.161.clone.1, s32[]{:T(128)} %constant.172.clone.1, s32[]{:T(128)} %constant.161.clone.1) | dynamic-update-slice | bytes 3276804 | tf_op jit(solution)/shard_map/scatter-add | solution.py:175
  188.6 3.7 constant_dynamic-update-slice_fusion
  193.1 5.9 %convolution_convert_fusion = bf16[64,128,400]{1,0,2:T(8,128)(2,1)S(1)} fusion(f32[8,32,400]{1,0,2:T(8,128)S(1)} %copy.121, s32[8]{0:T(128)S(1)} %copy-done.39, pred[8]{0:T(512)(128)(4,1)S(1)} %copy-done.34), kind=kOutput, calls=%fused_computation.3 | convolution fusion | flops 317850624 | bytes 6963240 | tf_op jit(solution)/shard_map/sj,jrh->srh/dot_general | solution.py:185
  199.0 16.0 %copy.191 = bf16[50,8,64,128]{3,1,2,0:T(8,128)(2,1)} copy(bf16[50,8,64,128]{3,2,1,0:T(8,128)(2,1)S(1)} %bitcast.238) | data formatting | bytes 13107200
  217.0 4.1 fusion.39
  221.2 45.7 %all-reduce.30.cloned.1.call-done = f32[3,400,400]{2,1,0:T(8,128)} async-done(((f32[3,400,400]{2,1,0:T(8,128)}), f32[3,400,400]{2,1,0:T(8,128)}) %all-reduce.30.cloned.1.call-update) | async-done | bytes 1920016
  266.9 2.3 constant_dynamic-slice_fusion.1
  269.2 35.3 %reduce-scatter.10.cloned.1.call-done = f32[200,400]{1,0:T(8,128)} async-done(((f32[800,400]{1,0:T(8,128)}), f32[200,400]{1,0:T(8,128)}) %reduce-scatter.10.cloned.1.call-update) | async-done | bytes 320016
  304.5 1.9 copy.117
  306.5 63.8 %reduce-scatter.8.cloned.1.call-done = bf16[1024,400]{0,1:T(8,128)(2,1)} async-done(((bf16[8192,400]{0,1:T(8,128)(2,1)}), bf16[1024,400]{0,1:T(8,128)(2,1)}) %reduce-scatter.8.cloned.1.call-update) | async-done | bytes 819216 | tf_op jit(solution)/shard_map/reduce_scatter | solution.py:186
  370.3 3.7 multiply_reduce_fusion.2
  375.5 2.2 fusion.94
  377.7 4.6 fusion.23
  382.3 34.9 %fusion = f32[800,112]{0,1:T(8,128)S(1)} fusion(f32[800,400]{0,1:T(8,128)} %fusion.94), kind=kCustom, calls=%all-reduce-scatter | all-reduce-scatter fusion | flops 358401 | bytes 1638912
  417.2 1.4 collective-permute-start
  418.7 2.6 collective-permute-done
  421.3 2.2 concatenate.18
  423.5 1.9 constant_dynamic-slice_fusion
  425.4 5.1 %convert_reduce_fusion = (f32[800]{0:T(1024)S(1)}, f32[1,1024,800]{1,2,0:T(8,128)}) fusion(bf16[1,1024,800]{1,2,0:T(8,128)(2,1)S(1)} %copy-done.14, f32[1024]{0:T(1024)S(1)} %broadcast_multiply_fusion.6, f32[1024]{0:T(1024)S(1)} %broadcast_multiply_fusion.8, bf16[1,1024,800]{1,2,0:T(8,128)(2,1)S(1)} %copy-done, f32[1024]{0:T(1024)S(1)} %broadcast_multiply_fusion.7, ...), kind=kLoop, calls=%fused_computation.5 | loop fusion | flops 9010400 | bytes 9853184 | tf_op jit(solution)/shard_map/reduce_sum | solution.py:141
  430.5 18.1 %all-reduce.25 = (f32[800]{0:T(1024)S(1)}, f32[800]{0:T(1024)S(1)}, f32[400]{0:T(512)S(1)}, f32[400]{0:T(512)S(1)}, f32[400]{0:T(512)S(1)}, /*index=5*/f32[400]{...) all-reduce(f32[800]{0:T(1024)S(1)} %get-tuple-element.50, ...), channel_id=6, replica_groups=mesh['ctx'=8,'wsh'=4] {'wsh'}, use_global_device_ids=true, to_apply=%region_21.22.clone | all-reduce | flops 4800 | bytes 38400
  449.3 12.6 %all-reduce.23 = (f32[200]{0:T(256)}, f32[200]{0:T(256)}, f32[100]{0:T(128)}, f32[100]{0:T(128)}, f32[100]{0:T(128)}, /*index=5*/f32[100]{0:T(128)}, f32[100]{0:T(128)}, f32[100]{0:T(128)}, f32[200]{0:T(256)}) all-reduce(f32[200]{0:T(256)S(1)} %dynamic-slice.37, ...), channel_id=1, replica_groups=mesh['ctx'=8,'wsh'=4] {'ctx'}, use_global_device_ids=true, to_apply=%region_22.23 | all-reduce | flops 1200 | bytes 9600 | tf_op jit(solution)/shard_map/psum | solution.py:223
  461.9 21.6 %all-reduce.32.cloned.1.call-done = (f32[800,100]{0,1:T(8,128)}, f32[3,400,100]{2,1,0:T(8,128)}, f32[400,200]{1,0:T(8,128)}) async-done(((f32[800,100]{0,1:T(8,128)}, f32[3,400,100]{2,1,0:T(8,128)}, f32[400,200]{1,0:T(8,128)}), (f32[800,100]{0,1:T(8,128)}, f32[3,400,100]{2,1,0:T(8,128)}, f32[400,200]{1,0:T(8,128)})) %all-reduce.32.cloned.1.call-update) | async-done | bytes 1120016 | tf_op jit(solution)/shard_map/psum | solution.py:223
  483.5 1.8 copy.207
  485.3 1.9 copy.208
  (160 shorter events, 16.4 us)
Async XLA Ops:
  7.2 32.7 %copy-start = (bf16[1,1024,800]{1,2,0:T(8,128)(2,1)S(1)}, bf16[1,1024,800]{1,2,0:T(8,128)(2,1)}, u32[]{:S(2)}) copy-start(bf16[1,1024,800]{1,2,0:T(8,128)(2,1)} %param.22) | copy-start | bytes 4915204
  7.2 130.4 %all-gather.4.cloned.1.call-start = ((), (), s32[]{:S(2)}) async-start(), calls=%async_computation.2 | async-start | bytes 7372800 | tf_op jit(solution)/shard_map/all_gather | solution.py:116
  38.1 96.5 %copy-start.24 = (f32[400]{0:T(512)}, f32[400]{0:T(512)S(1)}, u32[]{:S(2)}) copy-start(f32[400]{0:T(512)S(1)} %convert_element_type.82) | copy-start | bytes 4804
  38.1 19.4 %copy-start.20 = (f32[800]{0:T(1024)}, f32[800]{0:T(1024)S(1)}, u32[]{:S(2)}) copy-start(f32[800]{0:T(1024)S(1)} %convert_element_type.77) | copy-start | bytes 9604
  38.1 19.4 %copy-start.26 = (f32[800]{0:T(1024)}, f32[800]{0:T(1024)S(1)}, u32[]{:S(2)}) copy-start(f32[800]{0:T(1024)S(1)} %convert_element_type.78) | copy-start | bytes 9604
  38.1 2.3 copy-start.19
  40.4 18.4 %copy-start.22 = (f32[1024]{0:T(1024)}, f32[1024]{0:T(1024)S(1)}, u32[]{:S(2)}) copy-start(f32[1024]{0:T(1024)S(1)} %add_rsqrt_fusion.2) | copy-start | bytes 12292
  57.5 1.3 copy-start.16
  58.8 1.2 copy-start.10
  60.2 3.4 copy-start.28
  61.8 14.1 %copy-start.42 = (s32[64]{0:T(128)S(1)}, s32[64]{0:T(128)}, u32[]{:S(2)}) copy-start(s32[64]{0:T(128)} %param.25) | copy-start | bytes 772
  61.8 205.1 %all-reduce.30.cloned.1.call-start = ((), (), s32[]{:S(2)}) async-start(), calls=%async_computation.5 | async-start | bytes 4915200
  79.1 0.5 copy-start.38
  79.1 52.8 %copy-start.35 = (pred[8]{0:T(512)(128)(4,1)}, pred[8]{0:T(512)(128)(4,1)S(1)}, u32[]{:S(2)}) copy-start(pred[8]{0:T(512)(128)(4,1)S(1)} %get-tuple-element.99) | copy-start | bytes 28
  79.6 0.6 copy-start.33
  134.6 0.9 copy-start.8
  155.0 1.5 copy-start.2
  155.0 1.7 copy-start.4
  156.6 1.1 copy-start.3
  156.6 1.7 copy-start.12
  156.6 1.7 copy-start.29
  156.6 1.7 copy-start.30
  156.6 1.7 copy-start.32
  156.6 1.7 copy-start.37
  158.3 1.2 copy-start.15
  159.3 4.1 copy-start.1
  159.3 2.1 copy-start.13
  159.3 2.1 copy-start.31
  159.3 2.1 copy-start.41
  164.1 1.4 copy-start.7
  164.7 1.1 copy-start.6
  164.7 1.1 copy-start.36
  168.2 136.3 %reduce-scatter.10.cloned.1.call-start = ((), (), s32[]{:S(2)}) async-start(), calls=%async_computation.4 | async-start | bytes 2048000
  172.6 197.7 %reduce-scatter.8.cloned.1.call-start = ((), (), s32[]{:S(2)}) async-start(), calls=%async_computation.3 | async-start | bytes 7372800 | tf_op jit(solution)/shard_map/reduce_scatter | solution.py:186
  172.8 2.5 copy-start.9
  176.0 2.6 copy-start.5
  192.4 0.7 copy-start.34
  192.4 0.7 copy-start.39
  215.0 1.4 copy-start.40
  215.0 268.5 %all-reduce.32.cloned.1.call-start = ((), (), s32[]{:S(2)}) async-start(), calls=%async_computation.6 | async-start | bytes 2793472 | tf_op jit(solution)/shard_map/psum | solution.py:223
  221.1 149.2 %copy-start.25 = (f32[400]{0:T(512)S(1)}, f32[400]{0:T(512)}, u32[]{:S(2)}) copy-start(f32[400]{0:T(512)} %copy-done.24) | copy-start | bytes 4804
  374.0 1.4 copy-start.11
  375.5 2.2 copy-start.17
  375.5 2.2 copy-start.21
  375.5 2.2 copy-start.23
  375.5 2.2 copy-start.27
  417.2 4.1 collective-permute-start
  423.5 1.9 copy-start.14
  483.5 3.7 copy-start.18
Sparse Core Ops, SparseCore 0:
  61.9 46.2 all-gather.3
  168.4 98.4 all-reduce.29
  269.2 35.3 reduce-scatter.9
  308.2 62.0 reduce-scatter.7
  425.5 57.9 all-reduce.31
where the time goes:
time: 502 us; the launch traced here: 495 us
  waiting for transfers between devices  169 us (34%)
  blocking collectives  160 us (32%)
  local copies, waits for them, and re-layouts  81.9 us (16%)
  matrix products  36.4 us (7%)
  other arithmetic  28.1 us (6%)
  between operations  18 us (4%)
    unnamed x8, waiting for transfers between devices  83.7 us
    unnamed x3, blocking collectives  73.5 us
    reduce_scatter x1, waiting for transfers between devices, on_device(): lax.psum_scatter(spread.reshape(block_total * BLK, inner_width).astype(jn...  63.8 us
    unnamed x128, local copies, waits for them, and re-layouts  49.2 us
    all_gather x1, blocking collectives, on_device(): lax.all_gather(weight_conv, 'wsh', axis=2, tiled=True)  29.7 us
    psum x1, waiting for transfers between devices, on_device(): totals = lax.psum(tuple(shards), 'ctx')  21.6 us
    all_gather x1, blocking collectives, on_device(): lax.all_gather(weight_out, 'wsh', axis=1, tiled=True)  18.9 us
    all_gather x1, blocking collectives, on_device(): lax.all_gather(weight_in, 'wsh', axis=1, tiled=True)  16 us
  transfers between devices with their start and end apart: 6, of which 5 were waited for; matrix products, arithmetic and copies ran while one was open for 16% of the time, Pallas kernels for 0%

commit v1 on v0

v1 whole, which is shorter than its diff:
```python
import jax
import jax.numpy as jnp
from jax import lax
from jax.experimental import pallas as pl
from jax.experimental.pallas import tpu as pltpu
from jax.sharding import PartitionSpec as P

TAPS = 3
STEP = 16
BLK = 128
EDGE = (TAPS - 1) * STEP
EPS = 1e-05
LANES = 128
MESH = pl.DeviceIdType.MESH
F32 = jnp.float32
BF16 = jnp.bfloat16


def up(value, unit):
    return -(-value // unit) * unit


class Packed:
    def __init__(self, rows, panels, width, devices):
        self.rows, self.panels, self.width = rows, panels, width
        total = rows * panels
        if width % 4 == 0 and width > 64 and LANES - width >= width // 4 and total % 80 == 0:
            main, rest, quarter = total * 4 // 5, total // 5, width // 4
            self.parts = [(0, main, 0, width, 0, 0)]
            self.parts += [(main, rest, quarter * i, quarter, rest * i, width) for i in range(4)]
            used = main
        else:
            count = max(LANES // width, 1)
            used = up(-(-total // count), 16)
            self.parts = [
                (used * i, min(used, total - used * i), 0, width, 0, width * i)
                for i in range(count)
                if used * i < total
            ]
        self.used = used
        self.size = up(used, 16 * devices)

    def packed_spans(self):
        cuts = {0, self.used}
        for row, count, _, _, at, _ in self.parts:
            cuts |= {at, at + count}
            cuts |= {at + self.rows * h - row for h in range(self.panels) if row < self.rows * h < row + count}
        cuts = sorted(cuts)
        for start, end in zip(cuts, cuts[1:]):
            inside = []
            for row, count, column, columns, at, lane in self.parts:
                if at <= start and end <= at + count:
                    source = row + start - at
                    inside.append((source % self.rows, source // self.rows, column, columns, lane))
            yield start, end - start, sorted(inside, key=lambda item: item[-1])

    def plain_spans(self):
        cuts = {0, self.rows}
        for row, count, _, _, _, _ in self.parts:
            cuts |= {edge - self.rows * h for edge in (row, row + count) for h in range(self.panels)}
        cuts = sorted(cut for cut in cuts if 0 <= cut <= self.rows)
        for start, end in zip(cuts, cuts[1:]):
            panels = []
            for h in range(self.panels):
                first = self.rows * h + start
                inside = [
                    (column, at + first - row, lane, columns)
                    for row, count, column, columns, at, lane in self.parts
                    if row <= first < row + count
                ]
                panels.append([item[1:] for item in sorted(inside)])
            yield start, end - start, panels


def chunk_of(count):
    return next(size for size in (80, 64, 48, 32, 16) if count % size == 0)


def flip(value, mask):
    bit = 1
    out = value
    while bit <= mask:
        if mask & bit:
            out = out + bit - 2 * bit * ((value // bit) % 2)
        bit *= 2
    return out


def dot(a, b, contract=(1, 0)):
    return lax.dot_general(
        a, b, (((contract[0],), (contract[1],)), ((), ())), preferred_element_type=F32
    )


def dup(v, lanes):
    return jnp.concatenate([v] * (lanes // LANES), axis=1)


def fold_rows(v):
    out = v[0:8]
    for i in range(8, v.shape[0], 8):
        out = out + v[i : i + 8]
    return out


def fold_lanes(v):
    out = v[:, 0:LANES]
    for i in range(LANES, v.shape[1], LANES):
        out = out + v[:, i : i + LANES]
    return out


def total_rows(v):
    return jnp.sum(v, 0, keepdims=True)


class Copies:
    def __init__(self, send, recv):
        self.send, self.recv, self.count, self.open = send, recv, 0, []

    def start(self, source, target, device):
        copy = pltpu.make_async_remote_copy(
            src_ref=source,
            dst_ref=target,
            send_sem=self.send.at[self.count],
            recv_sem=self.recv.at[self.count],
            device_id=device,
            device_id_type=MESH,
        )
        self.count += 1
        self.open.append(copy)
        copy.start()
        return copy


LG = 256
FB = 80
CHUNKS = 2


def kernel(cfg, *refs):
    C, W, J, D, H = cfg["C"], cfg["W"], cfg["J"], cfg["D"], cfg["H"]
    forms, bases = cfg["forms"], cfg["bases"]
    width, vec_at = cfg["width"], cfg["vec_at"]
    half_chips = C // 2
    R = J * BLK
    CW = R // CHUNKS
    CJ = J // CHUNKS
    EW = CJ * EDGE
    (slots, tgt_ref, x_hbm, og_hbm, seg_ref, vec_ref, wi_ref, wc_ref, wo_ref) = refs[:9]
    (bo_hbm, ig_hbm, gi_ref, gc_ref, go_ref, vo_ref) = refs[9:15]
    (
        x_v, og_v, mu1, sc1, a1, h2, mu2, sc2, a2, b1, b2, a3, gv, gh, big, c3, g3,
        m1, m2, k1, k2, w_in, w_inT, w_cv, w_cvT, w_out, wps, vecb, sa, ta, ha, pt, nh,
        psg, rx1, rx2, s2, rx3, fo, p8, p4, acc8, acc4, vx, vr, vs, vz,
        lsem, ssem, rsem,
    ) = refs[15:]

    c = lax.axis_index("ctx")
    z = lax.axis_index("wsh")
    k = c % 2
    p = c // 2
    slot_in_order = k * half_chips + p
    sibling = (flip(c, 1), z)
    chips = [(flip(c, 2 * e), z) for e in range(1, half_chips)]
    planes = [(c, flip(z, d)) for d in range(1, W)]
    copies = Copies(ssem, rsem)
    shards = range(W)

    def local(i, source, target):
        copy = pltpu.make_async_copy(source, target, lsem.at[i])
        copy.start()
        return copy

    def loop(count, body):
        lax.fori_loop(0, count, lambda i, carry: (body(i), carry)[1], 0)

    bar = pltpu.get_barrier_semaphore()
    for m in range(1, C):
        pl.semaphore_signal(bar, inc=1, device_id=(flip(c, m), z), device_id_type=MESH)
    for device in planes:
        pl.semaphore_signal(bar, inc=1, device_id=device, device_id_type=MESH)
    x_copy = local(0, x_hbm, x_v)
    og_copy = local(1, og_hbm, og_v)
    sa[pl.ds(pl.multiple_of(c * J, 8), J)] = seg_ref[...]
    vecb[0] = vec_ref[...]
    acc8[...] = jnp.zeros_like(acc8)
    acc4[...] = jnp.zeros_like(acc4)
    vx[...] = jnp.zeros_like(vx)

    def pack(name, take, put, copies_of, dtype):
        form, base = forms[name], bases[name]
        for start, count, inside in form.packed_spans():
            size = chunk_of(count)

            def step(i, start=start, inside=inside, size=size):
                shift = i * size
                to = pl.ds(pl.multiple_of(base + start + shift, 16), size)
                for s in copies_of:
                    parts, lane = [], 0
                    for row, panel, column, columns, at in inside:
                        rows = pl.ds(pl.multiple_of(row + shift, 16), size)
                        parts.append(take(s, panel, rows, slice(column, column + columns)))
                        lane = at + columns
                    if lane < LANES:
                        parts.append(jnp.zeros((size, LANES - lane), dtype))
                    put(s, to, jnp.concatenate(parts, axis=1))

            loop(count // size, step)
        if form.size > form.used:
            for s in copies_of:
                rest = pl.ds(base + form.used, form.size - form.used)
                put(s, rest, jnp.zeros((form.size - form.used, LANES), dtype))

    def moved(columns, by):
        return slice(columns.start + by, columns.stop + by)

    def put_own(s, rows, value):
        wps[0, rows, :] = value

    own_shard = {
        "in": lambda s, panel, rows, columns: w_in[rows, columns],
        "conv": lambda s, panel, rows, columns: wc_ref[panel, rows, columns],
        "out": lambda s, panel, rows, columns: wo_ref[rows, moved(columns, width * panel)],
    }
    w_in[:, 0:width] = wi_ref[...].T
    for name, take in own_shard.items():
        pack(name, take, put_own, (0,), BF16)
    pl.semaphore_wait(bar, C - 1 + W - 1)

    vec_sends = [copies.start(vecb.at[0], vecb.at[d + 1], planes[d]) for d in range(W - 1)]

    def part(name, order):
        share = forms[name].size // C
        return pl.ds(pl.multiple_of(bases[name] + order * share, 16), share)

    def half(name, which):
        share = forms[name].size // 2
        return pl.ds(pl.multiple_of(bases[name] + which * share, 16), share)

    def z_send(name):
        rows = part(name, slot_in_order)
        return [copies.start(wps.at[0, rows], wps.at[d + 1, rows], planes[d]) for d in range(W - 1)]

    def plane_send(name, before):
        for copy in before:
            copy.wait_recv()
        there = wps.at[pl.ds(1, W - 1), part(name, slot_in_order)]
        return [copies.start(there, there, device) for device in chips]

    def sibling_send(name, before):
        for copy in before:
            copy.wait_recv()
        there = wps.at[pl.ds(1, W - 1), half(name, k)]
        return copies.start(there, there, sibling)

    w_z = {name: z_send(name) for name in forms}
    own_seg = sa.at[pl.ds(pl.multiple_of(c * J, 8), J)]
    seg_sends = [copies.start(own_seg, own_seg, (flip(c, m), z)) for m in range(1, C)]

    def unpack(name, target, stacked=False):
        form, base = forms[name], bases[name]
        for start, count, panels in form.plain_spans():
            size = chunk_of(count)
            groups = [[panel] for panel in panels] if stacked else [panels]
            for g, group in enumerate(groups):

                def step(i, first=g * form.rows + start, group=group, size=size):
                    shift = i * size
                    parts = [
                        wps[flip(z, s), pl.ds(pl.multiple_of(base + row + shift, 16), size), lane : lane + columns]
                        for s in shards
                        for panel in group
                        for row, lane, columns in panel
                    ]
                    target[pl.ds(pl.multiple_of(first + shift, 16), size), :] = jnp.concatenate(parts, axis=1)

                loop(count // size, step)

    def lanes_at(start):
        return pl.ds(pl.multiple_of(start, LG), LG)

    def blocks(n):
        return [slice(f, f + FB) for f in range(0, n, FB)]

    x_copy.wait()
    og_copy.wait()

    def first_stats(i):
        lanes = lanes_at(i * LG)
        acc = jnp.zeros((8, LG), F32)
        for f in blocks(D):
            acc += fold_rows(x_v[f, lanes].astype(F32))
            acc8[2, f] += fold_lanes(og_v[f, lanes].astype(F32))
        mean = total_rows(acc) * (1.0 / D)
        acc = jnp.zeros((8, LG), F32)
        for f in blocks(D):
            centred = x_v[f, lanes].astype(F32) - mean
            acc += fold_rows(centred * centred)
        mu1[:, lanes] = mean
        sc1[:, lanes] = lax.rsqrt(total_rows(acc) * (1.0 / D) + EPS)

    loop(R // LG, first_stats)

    for copy in vec_sends:
        copy.wait_recv()
    vecs = [vecb[flip(z, s)].astype(F32) for s in shards]
    narrow = jnp.concatenate([v[:, :width] for v in vecs], axis=1).T
    for i in range(6):
        scale = 0.5 if i < 4 else 1.0
        p4[i] = jnp.broadcast_to(narrow[:, 4 + i : 5 + i] * scale, (H, LANES))
    broad = jnp.concatenate(
        [
            jnp.concatenate([v[at + h : at + h + 1, :width] for v in vecs for h in range(2)], axis=1)
            for at in (0, 2, 10)
        ]
        + [jnp.zeros((5, D), F32)],
        axis=0,
    ).T
    for i in range(3):
        scale = 0.5 if i < 2 else 1.0
        p8[i] = jnp.broadcast_to(broad[:, i : i + 1] * scale, (D, LANES))

    def first_act(i):
        lanes = lanes_at(i * LG)
        mean, scaled = mu1[:, lanes], sc1[:, lanes]
        for f in blocks(D):
            normed = (x_v[f, lanes].astype(F32) - mean) * scaled
            pre = normed * dup(p8[0, f], LG) + dup(p8[1, f], LG)
            a1[f, lanes] = (pre * jnp.tanh(pre) + pre).astype(BF16)

    w_plane = {"in": plane_send("in", w_z["in"])}
    loop(R // LG // 2, first_act)
    w_plane["conv"] = plane_send("conv", w_z["conv"])
    loop(R // LG // 2, lambda i: first_act(i + R // LG // 2))
    w_plane["out"] = plane_send("out", w_z["out"])
    w_sib = {"in": sibling_send("in", w_plane["in"])}
    w_sib["in"].wait_recv()
    unpack("in", w_in)
    w_inT[...] = w_in[...].T

    def second(chunk):
        here = slice(chunk * CW, (chunk + 1) * CW)
        h2[:, here] = dot(w_inT[...], a1[:, here])

        def step(i):
            lanes = lanes_at(chunk * CW + i * LG)
            acc = jnp.zeros((8, LG), F32)
            for f in blocks(H):
                value = h2[f, lanes] + dup(p4[4, f], LG)
                h2[f, lanes] = value
                acc += fold_rows(value)
            mean = total_rows(acc) * (1.0 / H)
            acc = jnp.zeros((8, LG), F32)
            for f in blocks(H):
                centred = h2[f, lanes] - mean
                acc += fold_rows(centred * centred)
            scaled = lax.rsqrt(total_rows(acc) * (1.0 / H) + EPS)
            mu2[:, lanes] = mean
            sc2[:, lanes] = scaled
            for f in blocks(H):
                normed = (h2[f, lanes] - mean) * scaled
                pre = normed * dup(p4[0, f], LG) + dup(p4[1, f], LG)
                a2[f, lanes] = (pre * jnp.tanh(pre) + pre).astype(BF16)

        loop(CW // LG, step)

    def edge_send(store, source, chunk, first):
        lanes = slice(chunk * EW, (chunk + 1) * EW)
        store[c, :, lanes] = jnp.concatenate(
            [source[:, j * BLK + first : j * BLK + first + EDGE] for j in range(chunk * CJ, (chunk + 1) * CJ)], axis=1
        )
        there = store.at[c, :, lanes]
        return [copies.start(there, there, device) for device in chips], copies.start(there, there, sibling)

    def edge_forward(store, sends, chunk):
        lanes = slice(chunk * EW, (chunk + 1) * EW)
        passed = []
        for e in range(1, half_chips):
            there = store.at[flip(c, 2 * e), :, lanes]
            sends[e - 1].wait_recv()
            passed.append(copies.start(there, there, sibling))
        return passed

    def edge_take(store, waits, row, target):
        for copy in waits:
            copy.wait_recv()
        wanted = tgt_ref[row : row + 1, :]
        total = jnp.zeros((H, J * EDGE), F32)
        for device in range(C):
            ids = lax.broadcasted_iota(jnp.int32, (J * EDGE, J * EDGE), 0) + device * J * EDGE
            chosen = jnp.where(ids == wanted, 1.0, 0.0).astype(BF16)
            total += dot(store[device], chosen)
        target[...] = total.astype(BF16)

    t_first, t_near, t_passed = [], [], []
    for chunk in range(CHUNKS):
        second(chunk)
        sends, near = edge_send(ta, a2, chunk, BLK - EDGE)
        t_first.append(sends)
        t_near.append(near)
    w_sib["conv"] = sibling_send("conv", w_plane["conv"])
    w_sib["out"] = sibling_send("out", w_plane["out"])

    for copy in seg_sends:
        copy.wait_recv()
    own = sa[pl.ds(pl.multiple_of(c * J, 8), J)].astype(F32)

    def neighbour(first):
        out = []
        for j in range(J):
            row = sa[pl.ds(slots[first + j], 1), :].astype(F32)
            out.append(jnp.where(slots[first + 2 * J + j] > 0, row, -1.0))
        return jnp.concatenate(out, axis=0)

    before, behind = neighbour(0), neighbour(J)
    cut = BLK - STEP

    def same(a, b):
        return jnp.where(a == b, 1.0, 0.0)

    keep_1 = same(own, jnp.concatenate([before[:, cut:], own[:, :cut]], axis=1))
    keep_2 = same(own, jnp.concatenate([before[:, BLK - EDGE :], own[:, : BLK - EDGE]], axis=1))
    next_1 = same(behind[:, :EDGE], jnp.concatenate([own[:, cut:], behind[:, :STEP]], axis=1))
    next_2 = same(behind[:, :EDGE], own[:, BLK - EDGE :])
    for target, mask, size in ((m1, keep_1, BLK), (m2, keep_2, BLK), (k1, next_1, EDGE), (k2, next_2, EDGE)):
        for j in range(J):
            target[:, j * size : (j + 1) * size] = jnp.broadcast_to(mask[j : j + 1], (16, size)).astype(BF16)

    def tall(mask):
        return jnp.concatenate([mask] * (H // 16), axis=0)

    w_sib["conv"].wait_recv()
    unpack("conv", w_cv, stacked=True)
    for tap in range(TAPS):
        w_cvT[tap] = w_cv[tap * H : (tap + 1) * H].T
    w_sib["out"].wait_recv()
    unpack("out", w_out)
    for chunk in range(CHUNKS):
        t_passed += edge_forward(ta, t_first[chunk], chunk)
    for chunk in range(CHUNKS):
        here = slice(chunk * CW, (chunk + 1) * CW)
        g3[:, here] = dot(w_out[...], og_v[:, here])
    edge_take(ta, t_near + t_passed, 0, pt)

    def third(chunk):
        here = slice(chunk * CW, (chunk + 1) * CW)
        for j in range(chunk * CJ, (chunk + 1) * CJ):
            tile, edge = slice(j * BLK, (j + 1) * BLK), slice(j * EDGE, (j + 1) * EDGE)
            own, prev = a2[:, tile], pt[:, edge]
            b1[:, tile] = jnp.concatenate([prev[:, STEP:], own[:, :cut]], axis=1) * tall(m1[:, tile])
            b2[:, tile] = jnp.concatenate([prev, own[:, : BLK - EDGE]], axis=1) * tall(m2[:, tile])
        c3[:, here] = dot(w_cvT[0], a2[:, here]) + dot(w_cvT[1], b1[:, here]) + dot(w_cvT[2], b2[:, here])

        def step(i):
            lanes = lanes_at(chunk * CW + i * LG)
            acc = jnp.zeros((8, LG), F32)
            for f in blocks(H):
                value = c3[f, lanes] + dup(p4[5, f], LG)
                c3[f, lanes] = value
                acc += fold_rows(value)
            mean = total_rows(acc) * (1.0 / H)
            acc = jnp.zeros((8, LG), F32)
            for f in blocks(H):
                centred = c3[f, lanes] - mean
                acc += fold_rows(centred * centred)
            scaled = lax.rsqrt(total_rows(acc) * (1.0 / H) + EPS)
            first, second = jnp.zeros((8, LG), F32), jnp.zeros((8, LG), F32)
            for f in blocks(H):
                normed = (c3[f, lanes] - mean) * scaled
                gain = dup(p4[2, f], LG)
                pre = normed * gain + dup(p4[3, f], LG)
                t = jnp.tanh(pre)
                a3[f, lanes] = (pre * t + pre).astype(BF16)
                upstream = g3[f, lanes] * ((1.0 + t) * (1.0 + pre * (1.0 - t)))
                acc4[2, f] += fold_lanes(upstream * normed)
                acc4[3, f] += fold_lanes(upstream)
                upstream = upstream * gain
                g3[f, lanes] = upstream
                first += fold_rows(upstream)
                second += fold_rows(upstream * normed)
            first, second = total_rows(first) * (1.0 / H), total_rows(second) * (1.0 / H)
            for f in blocks(H):
                normed = (c3[f, lanes] - mean) * scaled
                grad = (scaled * (g3[f, lanes] - first - normed * second)).astype(BF16)
                gv[f, lanes] = grad
                acc4[5, f] += fold_lanes(grad.astype(F32))

        loop(CW // LG, step)

    h_first, h_near, h_passed = [], [], []
    for chunk in range(CHUNKS):
        third(chunk)
        sends, near = edge_send(ha, gv, chunk, 0)
        h_first.append(sends)
        h_near.append(near)

    taps_at = (c3, g3, big)
    whole_grad = {
        "in": lambda s, panel, rows, columns: big[rows, moved(columns, width * s)],
        "conv": lambda s, panel, rows, columns: taps_at[panel][rows, moved(columns, width * s)],
        "out": lambda s, panel, rows, columns: big[rows, moved(columns, width * (forms["out"].panels * s + panel))],
    }

    def put_grad(s, rows, value):
        psg[flip(z, s), rows, :] = value.astype(BF16)

    def pack_grad(name):
        pack(name, whole_grad[name], put_grad, shards, F32)

    def halved(name):
        return pl.ds(bases[name] // 2, forms[name].size // 2)

    def shared(name):
        return pl.ds(bases[name] // C, forms[name].size // C)

    def reduce_1(name):
        return copies.start(psg.at[:, half(name, 1 - k)], rx1.at[:, halved(name)], sibling)

    def tiles(rows, body):
        size = chunk_of(rows)
        loop(rows // size, lambda i: body(pl.multiple_of(i * size, 16), size))

    def reduce_2(name, before):
        before.wait_recv()
        form = forms[name]
        first, mine = bases[name] // 2, bases[name] + k * (form.size // 2)

        def add(at, size):
            to = pl.ds(pl.multiple_of(first + at, 16), size)
            here = pl.ds(pl.multiple_of(mine + at, 16), size)
            for d in range(W):
                psg[d, here] = (psg[d, here].astype(F32) + rx1[d, to].astype(F32)).astype(BF16)

        tiles(form.size // 2, add)
        share = form.size // C
        sends = []
        for e, device in enumerate(chips):
            rows = pl.ds(pl.multiple_of(mine + flip(p, e + 1) * share, 16), share)
            sends.append(copies.start(psg.at[:, rows], rx2.at[e, :, shared(name)], device))
        return sends

    def reduce_3(name, before):
        for copy in before:
            copy.wait_recv()
        share = forms[name].size // C
        first, mine = bases[name] // C, bases[name] + slot_in_order * share

        def add(at, size):
            to = pl.ds(pl.multiple_of(first + at, 16), size)
            here = pl.ds(pl.multiple_of(mine + at, 16), size)
            for d in range(W):
                total = psg[d, here].astype(F32)
                for e in range(half_chips - 1):
                    total = total + rx2[e, d, to].astype(F32)
                s2[d, to] = total.astype(BF16)

        tiles(share, add)
        return [copies.start(s2.at[d + 1, shared(name)], rx3.at[d, shared(name)], planes[d]) for d in range(W - 1)]

    def reduce_4(name, before):
        for copy in before:
            copy.wait_recv()
        share = forms[name].size // C
        first, mine = bases[name] // C, bases[name] + slot_in_order * share

        def add(at, size):
            to = pl.ds(pl.multiple_of(first + at, 16), size)
            total = s2[0, to].astype(F32)
            for d in range(W - 1):
                total = total + rx3[d, to].astype(F32)
            fo[pl.ds(pl.multiple_of(mine + at, 16), size)] = total

        tiles(share, add)
        there = fo.at[part(name, slot_in_order)]
        return [copies.start(there, there, device) for device in chips]

    def reduce_5(name, before):
        for copy in before:
            copy.wait_recv()
        there = fo.at[half(name, k)]
        return copies.start(there, there, sibling)

    def finish(name, before, target):
        before.wait_recv()
        form, base = forms[name], bases[name]
        pieces = []
        for start, count, panels in form.plain_spans():
            values = [
                [fo[base + row : base + row + count, lane : lane + columns] for row, lane, columns in panel]
                for panel in panels
            ]
            if name == "conv":
                for tap, parts in enumerate(values):
                    target[tap, start : start + count] = jnp.concatenate(parts, axis=1)
            else:
                pieces.append(jnp.concatenate(sum(values, []), axis=1))
                if name == "out":
                    target[start : start + count] = pieces[-1]
        if name == "in":
            target[...] = jnp.concatenate(pieces, axis=0).T

    big[0:H, 0:D] = dot(a3[...], og_v[...], (1, 1))
    pack_grad("out")
    g_out = reduce_1("out")
    for tap, source in enumerate((a2, b1, b2)):
        taps_at[tap][0:H, 0:H] = dot(source[...], gv[...], (1, 1))
    pack_grad("conv")
    g_conv = reduce_1("conv")
    for chunk in range(CHUNKS):
        h_passed += edge_forward(ha, h_first[chunk], chunk)
    g_out = reduce_2("out", g_out)
    g_conv = reduce_2("conv", g_conv)
    edge_take(ha, h_near + h_passed, 1, nh)

    def second_back(chunk):
        here = slice(chunk * CW, (chunk + 1) * CW)
        for j in range(chunk * CJ, (chunk + 1) * CJ):
            tile, edge = slice(j * BLK, (j + 1) * BLK), slice(j * EDGE, (j + 1) * EDGE)
            own, late = gv[:, tile], nh[:, edge]
            shifted = (late * tall(k1[:, edge]))[:, :STEP]
            b1[:, tile] = jnp.concatenate([(own * tall(m1[:, tile]))[:, STEP:], shifted], axis=1)
            shifted = late * tall(k2[:, edge])
            b2[:, tile] = jnp.concatenate([(own * tall(m2[:, tile]))[:, EDGE:], shifted], axis=1)
        c3[:, here] = (
            dot(w_cv[0:H], gv[:, here]) + dot(w_cv[H : 2 * H], b1[:, here]) + dot(w_cv[2 * H : 3 * H], b2[:, here])
        )

        def step(i):
            lanes = lanes_at(chunk * CW + i * LG)
            mean, scaled = mu2[:, lanes], sc2[:, lanes]
            first, second = jnp.zeros((8, LG), F32), jnp.zeros((8, LG), F32)
            for f in blocks(H):
                normed = (h2[f, lanes] - mean) * scaled
                gain = dup(p4[0, f], LG)
                pre = normed * gain + dup(p4[1, f], LG)
                t = jnp.tanh(pre)
                upstream = c3[f, lanes] * ((1.0 + t) * (1.0 + pre * (1.0 - t)))
                acc4[0, f] += fold_lanes(upstream * normed)
                acc4[1, f] += fold_lanes(upstream)
                upstream = upstream * gain
                c3[f, lanes] = upstream
                first += fold_rows(upstream)
                second += fold_rows(upstream * normed)
            first, second = total_rows(first) * (1.0 / H), total_rows(second) * (1.0 / H)
            for f in blocks(H):
                normed = (h2[f, lanes] - mean) * scaled
                grad = (scaled * (c3[f, lanes] - first - normed * second)).astype(BF16)
                gh[f, lanes] = grad
                acc4[4, f] += fold_lanes(grad.astype(F32))

        loop(CW // LG, step)

    for chunk in range(CHUNKS):
        second_back(chunk)
    big[:, 0:H] = dot(a1[...], gh[...], (1, 1))
    pack_grad("in")
    g_in = reduce_1("in")
    g_out = reduce_3("out", g_out)
    for side in range(D // H):
        w_cvT[side] = w_out[:, side * H : (side + 1) * H].T

    def first_back(chunk):
        here = slice(chunk * CW, (chunk + 1) * CW)
        big[:, here] = dot(w_in[...], gh[:, here])

        def step(i):
            lanes = lanes_at(chunk * CW + i * LG)
            mean, scaled = mu1[:, lanes], sc1[:, lanes]
            first, second = jnp.zeros((8, LG), F32), jnp.zeros((8, LG), F32)
            for f in blocks(D):
                normed = (x_v[f, lanes].astype(F32) - mean) * scaled
                gain = dup(p8[0, f], LG)
                pre = normed * gain + dup(p8[1, f], LG)
                t = jnp.tanh(pre)
                upstream = big[f, lanes] * ((1.0 + t) * (1.0 + pre * (1.0 - t)))
                acc8[0, f] += fold_lanes(upstream * normed)
                acc8[1, f] += fold_lanes(upstream)
                upstream = upstream * gain
                big[f, lanes] = upstream
                first += fold_rows(upstream)
                second += fold_rows(upstream * normed)
            first, second = total_rows(first) * (1.0 / D), total_rows(second) * (1.0 / D)
            for f in blocks(D):
                normed = (x_v[f, lanes].astype(F32) - mean) * scaled
                grad = scaled * (big[f, lanes] - first - normed * second)
                big[f, lanes] = og_v[f, lanes].astype(F32) + grad

        loop(CW // LG, step)
        return local(2 + chunk, big.at[:, here], ig_hbm.at[:, here])

    def last(chunk):
        here = slice(chunk * CW, (chunk + 1) * CW)
        for side, store in enumerate((c3, g3)):
            store[:, 0:CW] = dot(w_cvT[side], a3[:, here])

            def step(i, side=side, store=store):
                lanes, at = lanes_at(chunk * CW + i * LG), lanes_at(i * LG)
                for f in blocks(H):
                    to = slice(side * H + f.start, side * H + f.stop)
                    value = store[f, at] + dup(p8[2, to], LG)
                    x_v[to, lanes] = (x_v[to, lanes].astype(F32) + value).astype(BF16)

            loop(CW // LG, step)
        return local(4 + chunk, x_v.at[:, here], bo_hbm.at[:, here])

    out_copies = [first_back(0)]
    g_in = reduce_2("in", g_in)
    g_conv = reduce_3("conv", g_conv)
    out_copies.append(first_back(1))

    def row_sums(group, i, scale):
        return jnp.sum((acc8 if group == 8 else acc4)[i].T, 0, keepdims=True) * scale

    for (group, i, count, scale), at in vec_at:
        value = row_sums(group, i, scale)
        for t in range(-(-count // LANES)):
            size = min(LANES, count - t * LANES)
            vx[at + t : at + t + 1, 0:size] = value[:, t * LANES : t * LANES + size]
    vr[c] = vx[...]
    v_sends = [copies.start(vr.at[c], vr.at[c], (flip(c, m), z)) for m in range(1, C)]
    g_in = reduce_3("in", g_in)
    g_out = reduce_4("out", g_out)
    g_conv = reduce_4("conv", g_conv)
    out_copies.append(last(0))
    for copy in v_sends:
        copy.wait_recv()
    total = vr[0]
    for m in range(1, C):
        total = total + vr[m]
    vs[...] = total
    z_sends = [copies.start(vs, vz.at[d], planes[d]) for d in range(W - 1)]
    g_in = reduce_4("in", g_in)
    out_copies.append(last(1))
    g_out = reduce_5("out", g_out)
    g_conv = reduce_5("conv", g_conv)
    g_in = reduce_5("in", g_in)
    finish("out", g_out, go_ref)
    finish("conv", g_conv, gc_ref)
    for copy in z_sends:
        copy.wait_recv()
    total = vs[...]
    for d in range(W - 1):
        total = total + vz[d]
    vx[...] = total
    for row, ((_, _, count, _), at) in enumerate(vec_at):
        whole = jnp.concatenate([vx[at + t : at + t + 1] for t in range(-(-count // LANES))], axis=1)
        share = count // W
        mine = jnp.zeros((1, share), F32)
        for s in shards:
            mine = jnp.where(z == s, whole[:, s * share : (s + 1) * share], mine)
        vo_ref[row : row + 1, 0:share] = mine
    finish("in", g_in, gi_ref)
    for copy in copies.open:
        copy.wait_send()
    for copy in out_copies:
        copy.wait()


def on_device(
    block_in, out_grad, segments, block_deal, weight_in, weight_conv, weight_out,
    gain_first, shift_first, gain_second, shift_second, gain_third, shift_third, bias_first, bias_conv, bias_out,
):
    C, W = lax.axis_size("ctx"), lax.axis_size("wsh")
    _, rows, D = block_in.shape
    width = weight_in.shape[1]
    H = width * W
    panels = weight_out.shape[1] // width
    J = rows // BLK
    blocks = J * C
    forms = {
        "in": Packed(D, 1, width, C),
        "conv": Packed(H, TAPS, width, C),
        "out": Packed(H, panels, width, C),
    }
    bases, total = {}, 0
    for name, form in forms.items():
        bases[name] = total
        total += form.size

    device = lax.axis_index("ctx")
    mine = lax.dynamic_slice_in_dim(block_deal, device * J, J)
    wanted = jnp.concatenate([mine - 1, mine + 1])
    ids = jnp.arange(blocks, dtype=jnp.int32)
    found = jnp.sum(jnp.where(block_deal[None, :] == wanted[:, None], ids[None, :], 0), axis=1)
    there = jnp.logical_and(wanted >= 0, wanted < blocks)
    slots = jnp.concatenate([found, there.astype(jnp.int32)]).astype(jnp.int32)
    places = found.reshape(2, J, 1) * EDGE + jnp.arange(EDGE, dtype=jnp.int32)
    places = jnp.where(there.reshape(2, J, 1), places, -1).reshape(2, J * EDGE)

    vectors = [
        gain_first, shift_first, gain_second, shift_second, gain_third, shift_third, bias_first, bias_conv, bias_out,
    ]
    vec = jnp.concatenate([v.reshape(-1, width) for v in vectors], axis=0)
    vec = jnp.pad(vec, ((0, 16 - vec.shape[0]), (0, LANES - width)))

    vec_at, at = [], 0
    for item in [(8, 0, D, 0.5), (8, 1, D, 0.5), (8, 2, D, 1.0)] + [
        (4, i, H, 0.5 if i < 4 else 1.0) for i in range(6)
    ]:
        vec_at.append((item, at))
        at += -(-item[2] // LANES)
    v_rows = up(at, 8)
    cfg = {
        "C": C, "W": W, "J": J, "D": D, "H": H, "forms": forms, "bases": bases, "width": width, "vec_at": vec_at,
    }
    R = rows
    others = max(C // 2 - 1, 1)
    n_copies = (
        3 * ((W - 1) + (C // 2 - 1) + 1) + (W - 1) + (C - 1) + 2 * CHUNKS * (2 * (C // 2 - 1) + 1)
        + 3 * (2 * (C // 2 - 1) + (W - 1) + 2) + (C - 1) + (W - 1)
    )
    vmem = pltpu.VMEM
    scratch = [
        vmem((D, R), BF16),
        vmem((D, R), BF16),
        vmem((1, R), F32),
        vmem((1, R), F32),
        vmem((D, R), BF16),
        vmem((H, R), F32),
        vmem((1, R), F32),
        vmem((1, R), F32),
        vmem((H, R), BF16),
        vmem((H, R), BF16),
        vmem((H, R), BF16),
        vmem((H, R), BF16),
        vmem((H, R), BF16),
        vmem((H, R), BF16),
        vmem((D, R), F32),
        vmem((H, R), F32),
        vmem((H, R), F32),
        vmem((16, R), BF16),
        vmem((16, R), BF16),
        vmem((16, J * EDGE), BF16),
        vmem((16, J * EDGE), BF16),
        vmem((D, H), BF16),
        vmem((H, D), BF16),
        vmem((TAPS * H, H), BF16),
        vmem((TAPS, H, H), BF16),
        vmem((H, D), BF16),
        vmem((W, total, LANES), BF16),
        vmem((W, 16, LANES), BF16),
        vmem((blocks, BLK), jnp.int32),
        vmem((C, H, J * EDGE), BF16),
        vmem((C, H, J * EDGE), BF16),
        vmem((H, J * EDGE), BF16),
        vmem((H, J * EDGE), BF16),
        vmem((W, total, LANES), BF16),
        vmem((W, total // 2, LANES), BF16),
        vmem((others, W, total // C, LANES), BF16),
        vmem((W, total // C, LANES), BF16),
        vmem((W - 1, total // C, LANES), BF16),
        vmem((total, LANES), F32),
        vmem((3, D, LANES), F32),
        vmem((6, H, LANES), F32),
        vmem((3, D, LANES), F32),
        vmem((6, H, LANES), F32),
        vmem((v_rows, LANES), F32),
        vmem((C, v_rows, LANES), F32),
        vmem((v_rows, LANES), F32),
        vmem((W - 1, v_rows, LANES), F32),
        pltpu.SemaphoreType.DMA((6,)),
        pltpu.SemaphoreType.DMA((n_copies,)),
        pltpu.SemaphoreType.DMA((n_copies,)),
    ]
    any_spec = pl.BlockSpec(memory_space=pl.ANY)
    vmem_spec = pl.BlockSpec(memory_space=pltpu.VMEM)
    flat, tree = jax.tree.flatten(scratch)

    def run(*refs):
        kernel(cfg, *refs[:15], *jax.tree.unflatten(tree, refs[15:]))

    macs = R * (2 * D * H + TAPS * H * H) * 3
    bo, ig, gi, gc, go, vo = pl.pallas_call(
        run,
        out_shape=(
            jax.ShapeDtypeStruct((D, R), BF16),
            jax.ShapeDtypeStruct((D, R), F32),
            jax.ShapeDtypeStruct((width, D), F32),
            jax.ShapeDtypeStruct((TAPS, H, width), F32),
            jax.ShapeDtypeStruct((H, panels * width), F32),
            jax.ShapeDtypeStruct((16, up(panels * width, LANES)), F32),
        ),
        in_specs=[pl.BlockSpec(memory_space=pltpu.SMEM), vmem_spec, any_spec, any_spec] + [vmem_spec] * 5,
        out_specs=(any_spec, any_spec, vmem_spec, vmem_spec, vmem_spec, vmem_spec),
        scratch_shapes=flat,
        compiler_params=pltpu.CompilerParams(
            collective_id=0, has_side_effects=True, vmem_limit_bytes=62 * 2**20
        ),
        cost_estimate=pl.CostEstimate(
            flops=2 * macs, bytes_accessed=10 * R * D, transcendentals=2 * R * (D + 2 * H)
        ),
        name="block",
    )(
        slots,
        places,
        block_in[0].T,
        out_grad[0].T,
        segments.reshape(J, BLK),
        vec,
        weight_in.T,
        weight_conv,
        weight_out,
    )

    def own_share(index):
        return vo[index, : vec_at[index][0][2] // W]

    return (
        bo.T[None],
        ig.T[None],
        gi.T,
        gc,
        go,
        own_share(0), own_share(1), own_share(3), own_share(4), own_share(5), own_share(6),
        own_share(7), own_share(8), own_share(2),
    )


def solution(mesh):
    in_specs = (
        P("wsh", "ctx", None), P("wsh", "ctx", None), P("wsh", "ctx"), P(),
        P(None, "wsh"), P(None, None, "wsh"), P(None, "wsh"),
    ) + (P("wsh"),) * 9
    out_specs = (
        P("wsh", "ctx", None), P("wsh", "ctx", None),
        P(None, "wsh"), P(None, None, "wsh"), P(None, "wsh"),
    ) + (P("wsh"),) * 9
    return jax.shard_map(
        on_device, mesh=mesh, in_specs=in_specs, out_specs=out_specs, check_vma=False
    )
```

time: 502 us -> 97.4 us (0.19); the launches traced: 495 us -> 96.8 us
  waiting for transfers between devices: 169 us -> 0 us
  blocking collectives: 160 us -> 0 us
  Pallas kernels: 0 us -> 78.9 us
  local copies, waits for them, and re-layouts: 81.9 us -> 14.4 us
  matrix products: 36.4 us -> 0 us
  other arithmetic: 28.1 us -> 2.84 us
  between operations: 18 us -> 0.68 us
    unnamed x8 -> x0, waiting for transfers between devices: 83.7 us -> none
    pallas_call x0 -> x1, Pallas kernels: none -> 78.9 us  [on_device(): pl.pallas_call(run, out_shape=(jax.ShapeDtypeStruct((D, R), BF16), jax.Sh...]
    unnamed x3 -> x0, blocking collectives: 73.5 us -> none
    all_gather x4 -> x0, blocking collectives: 73.5 us -> none  [the longest x1 29.7 us: on_device(): lax.all_gather(weight_conv, 'wsh', axis=2, tiled=True)]
    reduce_scatter x1 -> x0, waiting for transfers between devices: 63.8 us -> none  [on_device(): lax.psum_scatter(spread.reshape(block_total * BLK, inner_width).astype(jn...]
    unnamed x128 -> x13, local copies, waits for them, and re-layouts: 49.2 us -> 6.91 us
    dot_general x15 -> x0, matrix products: 32 us -> none  [the longest x3 6.25 us: on_device(): jnp.einsum('jrg,hg->jrh', masked_grad, full_conv[kernel_tap_index], prefe...]
    psum x1 -> x0, waiting for transfers between devices: 21.6 us -> none  [on_device(): totals = lax.psum(tuple(shards), 'ctx')]
  transfers between devices with their start and end apart: 6 -> 0, of which waited for: 5 -> 0; matrix products, arithmetic and copies ran while one was open for 16% -> 0% of each run, Pallas kernels for 0% -> 0%
where the time goes in v1:
time: 97.4 us; the launch traced here: 96.8 us
  Pallas kernels  78.9 us (81%)
  local copies, waits for them, and re-layouts  14.4 us (15%)
  other arithmetic  2.84 us (3%)
    pallas_call x1, Pallas kernels, on_device(): pl.pallas_call(run, out_shape=(jax.ShapeDtypeStruct((D, R), BF16), jax.Sh...  78.9 us
    unnamed x13, local copies, waits for them, and re-layouts  6.91 us
    reshape x3, local copies, waits for them, and re-layouts, on_device(): vec = jnp.concatenate([v.reshape(-1, width) for v in vectors], axis=0)  2.21 us

profile of v1, /device:TPU:0, one launch (start us, length us, event | category | flops | bytes accessed | tf_op | source)
XLA Modules:
  0.0 96.8 jit_solution(16938231712104368774)
XLA Ops:
  0.6 0.7 broadcast_add_fusion.1
  1.4 0.1 and_convert_fusion
  1.5 0.8 select_reduce_fusion
  2.3 0.6 pad_add_fusion.1.refs_0_
  2.9 0.1 mul.16
  3.0 0.1 add.31
  3.0 0.1 add.32
  3.1 0.1 broadcast_in_dim.38
  3.2 0.1 broadcast_in_dim.39
  3.3 0.1 add.34
  3.4 0.6 add_select_fusion.refs_1_
  4.0 0.7 reshape.105
  4.7 0.7 reshape.106
  5.5 0.7 reshape.113
  6.2 1.4 %concatenate.27 = bf16[12,100]{1,0:T(8,128)(2,1)S(1)} concatenate(bf16[2,100]{1,0:T(2,128)(2,1)S(1)} %reshape.105, bf16[2,100]{1,0:T(2,128)(2,1)S(1)} %reshape.106, bf16[1,100]{1,0:T(2,128)(2,1)} %bitcast.46, bf16[1,100]{1,0:T(2,128)(2,1)} %bitcast.47, bf16[1,100]{1,0:T(2,128)(2,1)} %bitcast.48, bf16[1,100]{1,0:T(2,128)(2,1)} %bitcast.49, bf16[1,100]{1,0:T(2,128)(2,1)} %bitcast.50, ...), dimensions={0} | concatenate | bytes 4800 | tf_op jit(solution)/shard_map/concatenate | solution.py:794
  7.6 0.6 pad.4.refs_5_
  8.2 78.9 %block.1 = (bf16[800,1024]{1,0:T(8,128)(2,1)}, f32[800,1024]{1,0:T(8,128)}, f32[100,800]{1,0:T(8,128)}, f32[3,400,100]{2,1,0:T(8,128)}, f32[400,200]{1,0:T(8,128)}, /*index=5*/f32[16,256]{1,0:T(8,128)}) custom-call(s32[32]{0:T(128)} %pad_add_fusion.1.refs_0_, s32[2,256]{1,0:T(2,128)} %add_select_fusion.refs_1_, bf16[800,1024]{1,0:T(8,128)(2,1)} %bitcast.52, ...), custom_call_target="tpu_custom_call" | custom-call | flops 6881280000 | bytes 8192000 | tf_op jit(solution)/shard_map/block/pallas_call | solution.py:874
  87.1 1.4 %slice_bitcast_fusion = (f32[100]{0:T(128)}, f32[100]{0:T(128)}, f32[100]{0:T(128)}, f32[100]{0:T(128)}, f32[100]{0:T(128)}, /*index=5*/f32[100]{0:T(128)}) fusion(f32[16,256]{1,0:T(8,128)} %get-tuple-element.25), kind=kLoop, calls=%fused_computation.6 | loop fusion | bytes 4800 | tf_op jit(solution)/shard_map/squeeze | solution.py:907
  88.5 1.4 %fusion = (f32[1,200]{1,0:T(1,128)}, f32[1,200]{1,0:T(1,128)}, f32[1,200]{1,0:T(1,128)}) fusion(f32[16,256]{1,0:T(8,128)} %get-tuple-element.25), kind=kLoop, calls=%fused_computation.15 | loop fusion | bytes 4800 | tf_op jit(solution)/shard_map/slice | solution.py:907
  89.9 0.0 copy-start
  89.9 2.9 %copy.35 = bf16[1,1024,800]{1,2,0:T(8,128)(2,1)} copy(bf16[1,1024,800]{1,2,0:T(8,128)(2,1)} %bitcast.39) | data formatting | bytes 3276800
  92.7 0.0 copy-done
  92.7 0.0 copy-start.3
  92.8 0.0 copy-start.1
  92.8 1.7 %copy.36 = f32[1,1024,800]{1,2,0:T(8,128)} copy(f32[1,1024,800]{1,2,0:T(8,128)S(1)} %bitcast.38) | data formatting | bytes 6553600
  94.5 0.0 copy-done.3
  94.5 0.0 copy-start.2
  94.5 0.7 copy.37
  95.2 0.0 copy-done.1
  95.2 0.8 copy.38
  96.0 0.0 copy-done.2
  96.0 0.8 copy.39
  (3 shorter events, 0.0 us)
Async XLA Ops:
  89.9 2.9 %copy-start = (f32[800,1024]{1,0:T(8,128)S(1)}, f32[800,1024]{1,0:T(8,128)}, u32[]{:S(2)}) copy-start(f32[800,1024]{1,0:T(8,128)} %get-tuple-element.21) | copy-start | bytes 9830404
  92.7 1.7 %copy-start.3 = (f32[100,800]{1,0:T(8,128)S(1)}, f32[100,800]{1,0:T(8,128)}, u32[]{:S(2)}) copy-start(f32[100,800]{1,0:T(8,128)} %get-tuple-element.22) | copy-start | bytes 960004
  92.8 2.5 %copy-start.1 = (f32[3,400,100]{2,1,0:T(8,128)S(1)}, f32[3,400,100]{2,1,0:T(8,128)}, u32[]{:S(2)}) copy-start(f32[3,400,100]{2,1,0:T(8,128)} %get-tuple-element.56) | copy-start | bytes 1440004
  94.5 1.6 %copy-start.2 = (f32[400,200]{1,0:T(8,128)S(1)}, f32[400,200]{1,0:T(8,128)}, u32[]{:S(2)}) copy-start(f32[400,200]{1,0:T(8,128)} %get-tuple-element.57) | copy-start | bytes 960004

commit v2 on v1

--- a/solution.py
+++ b/solution.py
@@ -136,6 +136,7 @@
 LG = 256
 FB = 80
 CHUNKS = 2
+SPREAD = 5
 
 
 def kernel(cfg, *refs):
@@ -147,14 +148,15 @@
     CW = R // CHUNKS
     CJ = J // CHUNKS
     EW = CJ * EDGE
-    (slots, tgt_ref, x_hbm, og_hbm, seg_ref, vec_ref, wi_ref, wc_ref, wo_ref) = refs[:9]
-    (bo_hbm, ig_hbm, gi_ref, gc_ref, go_ref, vo_ref) = refs[9:15]
+    (deal, x_hbm, og_hbm, seg_ref, wi_ref, wc_ref, wo_ref) = refs[:7]
+    vec_refs = refs[7:16]
+    (bo_hbm, ig_hbm, fo_hbm, vo_ref) = refs[16:20]
     (
         x_v, og_v, mu1, sc1, a1, h2, mu2, sc2, a2, b1, b2, a3, gv, gh, big, c3, g3,
         m1, m2, k1, k2, w_in, w_inT, w_cv, w_cvT, w_out, wps, vecb, sa, ta, ha, pt, nh,
         psg, rx1, rx2, s2, rx3, fo, p8, p4, acc8, acc4, vx, vr, vs, vz,
         lsem, ssem, rsem,
-    ) = refs[15:]
+    ) = refs[20:]
 
     c = lax.axis_index("ctx")
     z = lax.axis_index("wsh")
@@ -183,10 +185,6 @@
     x_copy = local(0, x_hbm, x_v)
     og_copy = local(1, og_hbm, og_v)
     sa[pl.ds(pl.multiple_of(c * J, 8), J)] = seg_ref[...]
-    vecb[0] = vec_ref[...]
-    acc8[...] = jnp.zeros_like(acc8)
-    acc4[...] = jnp.zeros_like(acc4)
-    vx[...] = jnp.zeros_like(vx)
 
     def pack(name, take, put, copies_of, dtype):
         form, base = forms[name], bases[name]
@@ -223,13 +221,6 @@
         "conv": lambda s, panel, rows, columns: wc_ref[panel, rows, columns],
         "out": lambda s, panel, rows, columns: wo_ref[rows, moved(columns, width * panel)],
     }
-    w_in[:, 0:width] = wi_ref[...].T
-    for name, take in own_shard.items():
-        pack(name, take, put_own, (0,), BF16)
-    pl.semaphore_wait(bar, C - 1 + W - 1)
-
-    vec_sends = [copies.start(vecb.at[0], vecb.at[d + 1], planes[d]) for d in range(W - 1)]
-
     def part(name, order):
         share = forms[name].size // C
         return pl.ds(pl.multiple_of(bases[name] + order * share, 16), share)
@@ -254,9 +245,28 @@
         there = wps.at[pl.ds(1, W - 1), half(name, k)]
         return copies.start(there, there, sibling)
 
-    w_z = {name: z_send(name) for name in forms}
+    w_in[:, 0:width] = wi_ref[...].T
+    pack("in", own_shard["in"], put_own, (0,), BF16)
+    rows = []
+    for ref in vec_refs:
+        row = ref[...].astype(F32).reshape(1, ref.shape[0])
+        for h in range(ref.shape[0] // width):
+            rows.append(
+                jnp.concatenate([row[:, h * width : (h + 1) * width], jnp.zeros((1, LANES - width), F32)], axis=1)
+            )
+    rows.append(jnp.zeros((16 - len(rows), LANES), F32))
+    vecb[0] = jnp.concatenate(rows, axis=0).astype(BF16)
+    pl.semaphore_wait(bar, C - 1 + W - 1)
+    vec_sends = [copies.start(vecb.at[0], vecb.at[d + 1], planes[d]) for d in range(W - 1)]
+    w_z = {"in": z_send("in")}
+    for name in ("conv", "out"):
+        pack(name, own_shard[name], put_own, (0,), BF16)
+        w_z[name] = z_send(name)
     own_seg = sa.at[pl.ds(pl.multiple_of(c * J, 8), J)]
     seg_sends = [copies.start(own_seg, own_seg, (flip(c, m), z)) for m in range(1, C)]
+    acc8[...] = jnp.zeros_like(acc8)
+    acc4[...] = jnp.zeros_like(acc4)
+    vx[...] = jnp.zeros_like(vx)
 
     def unpack(name, target, stacked=False):
         form, base = forms[name], bases[name]
@@ -382,16 +392,39 @@
             passed.append(copies.start(there, there, sibling))
         return passed
 
-    def edge_take(store, waits, row, target):
+    mine = [deal[c * J + j] for j in range(J)]
+    edge_lane = lax.broadcasted_iota(jnp.int32, (1, J * EDGE), 1)
+    edge_block = jnp.zeros((1, J * EDGE), jnp.int32)
+    seg_block = jnp.zeros((J, BLK), jnp.int32)
+    for j in range(J):
+        inside = jnp.logical_and(edge_lane >= j * EDGE, edge_lane < (j + 1) * EDGE)
+        edge_block = jnp.where(inside, mine[j], edge_block)
+        seg_block = jnp.where(lax.broadcasted_iota(jnp.int32, (J, BLK), 0) == j, mine[j], seg_block)
+    diagonal = jnp.where(
+        lax.broadcasted_iota(jnp.int32, (EDGE, J * EDGE), 0)
+        == lax.broadcasted_iota(jnp.int32, (EDGE, J * EDGE), 1) % EDGE,
+        1.0,
+        0.0,
+    )
+
+    def edge_take(store, waits, step, target):
         for copy in waits:
             copy.wait_recv()
-        wanted = tgt_ref[row : row + 1, :]
+        wanted = edge_block + step
         total = jnp.zeros((H, J * EDGE), F32)
         for device in range(C):
-            ids = lax.broadcasted_iota(jnp.int32, (J * EDGE, J * EDGE), 0) + device * J * EDGE
-            chosen = jnp.where(ids == wanted, 1.0, 0.0).astype(BF16)
-            total += dot(store[device], chosen)
+            chosen = [
+                diagonal * jnp.where(wanted == deal[device * J + j], 1.0, 0.0) for j in range(J)
+            ]
+            total += dot(store[device], jnp.concatenate(chosen, axis=0).astype(BF16))
         target[...] = total.astype(BF16)
+
+    def seg_take(step):
+        wanted = seg_block + step
+        out = jnp.full((J, BLK), -1, jnp.int32)
+        for slot in range(C * J):
+            out = jnp.where(wanted == deal[slot], jnp.broadcast_to(sa[slot : slot + 1], (J, BLK)), out)
+        return out
 
     t_first, t_near, t_passed = [], [], []
     for chunk in range(CHUNKS):
@@ -404,16 +437,7 @@
 
     for copy in seg_sends:
         copy.wait_recv()
-    own = sa[pl.ds(pl.multiple_of(c * J, 8), J)].astype(F32)
-
-    def neighbour(first):
-        out = []
-        for j in range(J):
-            row = sa[pl.ds(slots[first + j], 1), :].astype(F32)
-            out.append(jnp.where(slots[first + 2 * J + j] > 0, row, -1.0))
-        return jnp.concatenate(out, axis=0)
-
-    before, behind = neighbour(0), neighbour(J)
+    own, before, behind = sa[pl.ds(pl.multiple_of(c * J, 8), J)], seg_take(-1), seg_take(1)
     cut = BLK - STEP
 
     def same(a, b):
@@ -441,7 +465,7 @@
     for chunk in range(CHUNKS):
         here = slice(chunk * CW, (chunk + 1) * CW)
         g3[:, here] = dot(w_out[...], og_v[:, here])
-    edge_take(ta, t_near + t_passed, 0, pt)
+    edge_take(ta, t_near + t_passed, -1, pt)
 
     def third(chunk):
         here = slice(chunk * CW, (chunk + 1) * CW)
@@ -581,25 +605,6 @@
         there = fo.at[half(name, k)]
         return copies.start(there, there, sibling)
 
-    def finish(name, before, target):
-        before.wait_recv()
-        form, base = forms[name], bases[name]
-        pieces = []
-        for start, count, panels in form.plain_spans():
-            values = [
-                [fo[base + row : base + row + count, lane : lane + columns] for row, lane, columns in panel]
-                for panel in panels
-            ]
-            if name == "conv":
-                for tap, parts in enumerate(values):
-                    target[tap, start : start + count] = jnp.concatenate(parts, axis=1)
-            else:
-                pieces.append(jnp.concatenate(sum(values, []), axis=1))
-                if name == "out":
-                    target[start : start + count] = pieces[-1]
-        if name == "in":
-            target[...] = jnp.concatenate(pieces, axis=0).T
-
     big[0:H, 0:D] = dot(a3[...], og_v[...], (1, 1))
     pack_grad("out")
     g_out = reduce_1("out")
@@ -735,26 +740,80 @@
     g_out = reduce_5("out", g_out)
     g_conv = reduce_5("conv", g_conv)
     g_in = reduce_5("in", g_in)
-    finish("out", g_out, go_ref)
-    finish("conv", g_conv, gc_ref)
     for copy in z_sends:
         copy.wait_recv()
     total = vs[...]
     for d in range(W - 1):
         total = total + vz[d]
-    vx[...] = total
-    for row, ((_, _, count, _), at) in enumerate(vec_at):
-        whole = jnp.concatenate([vx[at + t : at + t + 1] for t in range(-(-count // LANES))], axis=1)
-        share = count // W
-        mine = jnp.zeros((1, share), F32)
-        for s in shards:
-            mine = jnp.where(z == s, whole[:, s * share : (s + 1) * share], mine)
-        vo_ref[row : row + 1, 0:share] = mine
-    finish("in", g_in, gi_ref)
+    vo_ref[...] = total
+    for copy in (g_out, g_conv, g_in):
+        copy.wait_recv()
+    out_copies.append(local(0, fo, fo_hbm))
     for copy in copies.open:
         copy.wait_send()
     for copy in out_copies:
         copy.wait()
+
+
+def spread(cfg, *refs):
+    W, forms, bases, width, vec_at = (cfg[key] for key in ("W", "forms", "bases", "width", "vec_at"))
+    bo_in, ig_in, fo_in, vx, bo_out, ig_out, gi_out, gc_out, go_out = refs[:9]
+    vec_out, (ig_v, bo_v, fo, gi, gc, go, sem) = refs[9:18], refs[18:]
+    z = lax.axis_index("wsh")
+    used = 0
+
+    def copy(source, target):
+        nonlocal used
+        used += 1
+        move = pltpu.make_async_copy(source, target, sem.at[used - 1])
+        move.start()
+        return move
+
+    grads = copy(fo_in, fo)
+    pieces = []
+    for source, stage, target in ((ig_in, ig_v, ig_out), (bo_in, bo_v, bo_out)):
+        size = source.shape[0] // SPREAD
+        for i in range(SPREAD):
+            rows = pl.ds(i * size, size)
+            pieces.append((copy(source.at[rows], stage.at[rows]), stage.at[rows], target.at[rows]))
+    moves = []
+
+    def pass_on(count):
+        for come, stage, target in pieces[:count]:
+            come.wait()
+            moves.append(copy(stage, target))
+        del pieces[:count]
+
+    for ((_, _, count, _), at), target in zip(vec_at, vec_out):
+        whole = jnp.concatenate([vx[at + t : at + t + 1] for t in range(-(-count // LANES))], axis=1)
+        share = count // W
+        mine = jnp.zeros((1, share), F32)
+        for s in range(W):
+            mine = jnp.where(z == s, whole[:, s * share : (s + 1) * share], mine)
+        target[...] = mine.reshape(share)
+    grads.wait()
+    pass_on(2)
+    for name, stage, target in (("conv", gc, gc_out), ("out", go, go_out), ("in", gi, gi_out)):
+        form, base, parts = forms[name], bases[name], []
+        for start, count, panels in form.plain_spans():
+            values = [
+                [fo[base + row : base + row + count, lane : lane + columns] for row, lane, columns in panel]
+                for panel in panels
+            ]
+            if name == "conv":
+                for tap, part in enumerate(values):
+                    stage[tap, start : start + count] = jnp.concatenate(part, axis=1)
+            else:
+                parts.append(jnp.concatenate(sum(values, []), axis=1))
+                if name == "out":
+                    stage[start : start + count] = parts[-1]
+        if name == "in":
+            stage[...] = jnp.concatenate(parts, axis=0).T
+        moves.append(copy(stage, target))
+        pass_on(2)
+    pass_on(len(pieces))
+    for move in moves:
+        move.wait()
 
 
 def on_device(
@@ -767,7 +826,6 @@
     H = width * W
     panels = weight_out.shape[1] // width
     J = rows // BLK
-    blocks = J * C
     forms = {
         "in": Packed(D, 1, width, C),
         "conv": Packed(H, TAPS, width, C),
@@ -777,22 +835,6 @@
     for name, form in forms.items():
         bases[name] = total
         total += form.size
-
-    device = lax.axis_index("ctx")
-    mine = lax.dynamic_slice_in_dim(block_deal, device * J, J)
-    wanted = jnp.concatenate([mine - 1, mine + 1])
-    ids = jnp.arange(blocks, dtype=jnp.int32)
-    found = jnp.sum(jnp.where(block_deal[None, :] == wanted[:, None], ids[None, :], 0), axis=1)
-    there = jnp.logical_and(wanted >= 0, wanted < blocks)
-    slots = jnp.concatenate([found, there.astype(jnp.int32)]).astype(jnp.int32)
-    places = found.reshape(2, J, 1) * EDGE + jnp.arange(EDGE, dtype=jnp.int32)
-    places = jnp.where(there.reshape(2, J, 1), places, -1).reshape(2, J * EDGE)
-
-    vectors = [
-        gain_first, shift_first, gain_second, shift_second, gain_third, shift_third, bias_first, bias_conv, bias_out,
-    ]
-    vec = jnp.concatenate([v.reshape(-1, width) for v in vectors], axis=0)
-    vec = jnp.pad(vec, ((0, 16 - vec.shape[0]), (0, LANES - width)))
 
     vec_at, at = [], 0
     for item in [(8, 0, D, 0.5), (8, 1, D, 0.5), (8, 2, D, 1.0)] + [
@@ -840,7 +882,7 @@
         vmem((H, D), BF16),
         vmem((W, total, LANES), BF16),
         vmem((W, 16, LANES), BF16),
-        vmem((blocks, BLK), jnp.int32),
+        vmem((J * C, BLK), jnp.int32),
         vmem((C, H, J * EDGE), BF16),
         vmem((C, H, J * EDGE), BF16),
         vmem((H, J * EDGE), BF16),
@@ -868,21 +910,19 @@
     flat, tree = jax.tree.flatten(scratch)
 
     def run(*refs):
-        kernel(cfg, *refs[:15], *jax.tree.unflatten(tree, refs[15:]))
+        kernel(cfg, *refs[:20], *jax.tree.unflatten(tree, refs[20:]))
 
     macs = R * (2 * D * H + TAPS * H * H) * 3
-    bo, ig, gi, gc, go, vo = pl.pallas_call(
+    bo, ig, fo, vo = pl.pallas_call(
         run,
         out_shape=(
             jax.ShapeDtypeStruct((D, R), BF16),
             jax.ShapeDtypeStruct((D, R), F32),
-            jax.ShapeDtypeStruct((width, D), F32),
-            jax.ShapeDtypeStruct((TAPS, H, width), F32),
-            jax.ShapeDtypeStruct((H, panels * width), F32),
-            jax.ShapeDtypeStruct((16, up(panels * width, LANES)), F32),
+            jax.ShapeDtypeStruct((total, LANES), F32),
+            jax.ShapeDtypeStruct((v_rows, LANES), F32),
         ),
-        in_specs=[pl.BlockSpec(memory_space=pltpu.SMEM), vmem_spec, any_spec, any_spec] + [vmem_spec] * 5,
-        out_specs=(any_spec, any_spec, vmem_spec, vmem_spec, vmem_spec, vmem_spec),
+        in_specs=[pl.BlockSpec(memory_space=pltpu.SMEM), any_spec, any_spec] + [vmem_spec] * 13,
+        out_specs=(any_spec, any_spec, any_spec, vmem_spec),
         scratch_shapes=flat,
         compiler_params=pltpu.CompilerParams(
             collective_id=0, has_side_effects=True, vmem_limit_bytes=62 * 2**20
@@ -892,29 +932,39 @@
         ),
         name="block",
     )(
-        slots,
-        places,
+        block_deal,
         block_in[0].T,
         out_grad[0].T,
         segments.reshape(J, BLK),
-        vec,
         weight_in.T,
         weight_conv,
         weight_out,
+        gain_first, shift_first, gain_second, shift_second, gain_third, shift_third, bias_first, bias_conv, bias_out,
     )
-
-    def own_share(index):
-        return vo[index, : vec_at[index][0][2] // W]
-
-    return (
-        bo.T[None],
-        ig.T[None],
-        gi.T,
-        gc,
-        go,
-        own_share(0), own_share(1), own_share(3), own_share(4), own_share(5), own_share(6),
-        own_share(7), own_share(8), own_share(2),
-    )
+    results = pl.pallas_call(
+        lambda *refs: spread(cfg, *refs),
+        out_shape=(
+            jax.ShapeDtypeStruct((D, R), BF16),
+            jax.ShapeDtypeStruct((D, R), F32),
+            jax.ShapeDtypeStruct((width, D), F32),
+            jax.ShapeDtypeStruct((TAPS, H, width), F32),
+            jax.ShapeDtypeStruct((H, panels * width), F32),
+        )
+        + tuple(jax.ShapeDtypeStruct((item[2] // W,), F32) for item, _ in vec_at),
+        in_specs=[any_spec, any_spec, any_spec, vmem_spec],
+        out_specs=(any_spec,) * 5 + (vmem_spec,) * 9,
+        scratch_shapes=[
+            vmem((D, R), F32), vmem((D, R), BF16), vmem((total, LANES), F32),
+            vmem((width, D), F32), vmem((TAPS, H, width), F32), vmem((H, panels * width), F32),
+            pltpu.SemaphoreType.DMA((4 * SPREAD + 4,)),
+        ],
+        compiler_params=pltpu.CompilerParams(vmem_limit_bytes=62 * 2**20),
+        cost_estimate=pl.CostEstimate(flops=0, bytes_accessed=14 * R * D, transcendentals=0),
+        name="spread",
+    )(bo, ig, fo, vo)
+    bo, ig, gi, gc, go = results[:5]
+    vec = results[5:]
+    return (bo.T[None], ig.T[None], gi.T, gc, go, vec[0], vec[1], *vec[3:], vec[2])
 
 
 def solution(mesh):

time: 97.4 us -> 86 us (0.88)
  local copies, waits for them, and re-layouts: 14.4 us -> 0 us
  Pallas kernels: 78.9 us -> 84.2 us
  other arithmetic: 2.84 us -> 0 us
    unnamed x13 -> x0, local copies, waits for them, and re-layouts: 6.91 us -> none
    pallas_call x0 -> x1, Pallas kernels: none -> 5.92 us  [on_device(): pl.pallas_call(lambda *refs: spread(cfg, *refs), out_shape=(jax.ShapeDtyp...]
    reshape x3 -> x0, local copies, waits for them, and re-layouts: 2.21 us -> none  [on_device(): vec = jnp.concatenate([v.reshape(-1, width) for v in vectors], axis=0)]
    concatenate x1 -> x0, local copies, waits for them, and re-layouts: 1.42 us -> none  [on_device(): vec = jnp.concatenate([v.reshape(-1, width) for v in vectors], axis=0)]
    squeeze x1 -> x0, local copies, waits for them, and re-layouts: 1.4 us -> none  [own_share(): return vo[index, :vec_at[index][0][2] // W]]
    slice x1 -> x0, local copies, waits for them, and re-layouts: 1.38 us -> none  [own_share(): return vo[index, :vec_at[index][0][2] // W]]
where the time goes in v2:
time: 86 us; the launch traced here: 85 us
  Pallas kernels  84.2 us (98%)
    pallas_call x1, Pallas kernels, on_device(): pl.pallas_call(run, out_shape=(jax.ShapeDtypeStruct((D, R), BF16), jax.Sh...  78.2 us
    pallas_call x1, Pallas kernels, on_device(): pl.pallas_call(lambda *refs: spread(cfg, *refs), out_shape=(jax.ShapeDtyp...  5.92 us

profile of v2, /device:TPU:0, one launch (start us, length us, event | category | flops | bytes accessed | tf_op | source)
XLA Modules:
  0.0 85.0 jit_solution(12019065361763655412)
XLA Ops:
  0.7 78.2 %block.1 = (bf16[800,1024]{1,0:T(8,128)(2,1)}, f32[800,1024]{1,0:T(8,128)}, f32[2304,128]{1,0:T(8,128)}, f32[48,128]{1,0:T(8,128)}) custom-call(s32[64]{0:T(128)} %refs_0_.1, bf16[800,1024]{1,0:T(8,128)(2,1)} %bitcast.16, bf16[800,1024]{1,0:T(8,128)(2,1)} %bitcast.17, s32[8,128]{1,0:T(8,128)} %bitcast.21, bf16[100,800]{1,0:T(8,128)(2,1)} %bitcast.20, ...), custom_call_target="tpu_custom_call" | custom-call | flops 6881280000 | bytes 8192000 | tf_op jit(solution)/shard_map/block/pallas_call | solution.py:916
  78.9 5.9 %spread.1 = (bf16[800,1024]{1,0:T(8,128)(2,1)}, f32[800,1024]{1,0:T(8,128)}, f32[100,800]{1,0:T(8,128)}, f32[3,400,100]{2,1,0:T(8,128)}, f32[400,200]{1,0:T(8,12...) custom-call(bf16[800,1024]{1,0:T(8,128)(2,1)} %get-tuple-element.32., ...), custom_call_target="tpu_custom_call" | custom-call | bytes 11468800 | tf_op jit(solution)/shard_map/spread/pallas_call | solution.py:944

commit v3 on v2

--- a/solution.py
+++ b/solution.py
@@ -114,27 +114,38 @@
     return jnp.sum(v, 0, keepdims=True)
 
 
+class Group:
+    def __init__(self, send, recv, moves, size):
+        self.send, self.recv, self.size = send, recv, size
+        for source, target, device in moves:
+            pltpu.make_async_remote_copy(
+                src_ref=source,
+                dst_ref=target,
+                send_sem=send,
+                recv_sem=recv,
+                device_id=device,
+                device_id_type=MESH,
+            ).start()
+
+    def wait(self):
+        pltpu.make_async_copy(self.size, self.size, self.recv).wait()
+
+    def wait_sent(self):
+        pltpu.make_async_copy(self.size, self.size, self.send).wait()
+
+
 class Copies:
     def __init__(self, send, recv):
-        self.send, self.recv, self.count, self.open = send, recv, 0, []
-
-    def start(self, source, target, device):
-        copy = pltpu.make_async_remote_copy(
-            src_ref=source,
-            dst_ref=target,
-            send_sem=self.send.at[self.count],
-            recv_sem=self.recv.at[self.count],
-            device_id=device,
-            device_id_type=MESH,
-        )
-        self.count += 1
-        self.open.append(copy)
-        copy.start()
-        return copy
-
-
-LG = 256
-FB = 80
+        self.send, self.recv, self.groups = send, recv, []
+
+    def start(self, moves, size):
+        n = len(self.groups)
+        self.groups.append(Group(self.send.at[n], self.recv.at[n], moves, size))
+        return self.groups[-1]
+
+
+LG = 512
+FB = 16
 CHUNKS = 2
 SPREAD = 5
 
@@ -148,14 +159,14 @@
     CW = R // CHUNKS
     CJ = J // CHUNKS
     EW = CJ * EDGE
-    (deal, x_hbm, og_hbm, seg_ref, wi_ref, wc_ref, wo_ref) = refs[:7]
-    vec_refs = refs[7:16]
+    (deal, x_hbm, og_hbm, seg_hbm, wi_hbm, wc_hbm, wo_hbm) = refs[:7]
+    vec_hbm = refs[7:16]
     (bo_hbm, ig_hbm, fo_hbm, vo_ref) = refs[16:20]
     (
-        x_v, og_v, mu1, sc1, a1, h2, mu2, sc2, a2, b1, b2, a3, gv, gh, big, c3, g3,
+        x_v, og_v, mu1, sc1, a1, h2, mu2, sc2, bb, a3, gv, gh, big, c3, g3,
         m1, m2, k1, k2, w_in, w_inT, w_cv, w_cvT, w_out, wps, vecb, sa, ta, ha, pt, nh,
-        psg, rx1, rx2, s2, rx3, fo, p8, p4, acc8, acc4, vx, vr, vs, vz,
-        lsem, ssem, rsem,
+        psg, rx1, rx2, s2, rx3, rz, tz, fo, p8, p4, acc8, acc4, vx, vr, vs, vz,
+        wi_ref, wc_ref, wo_ref, *vec_refs, lsem, ssem, rsem,
     ) = refs[20:]
 
     c = lax.axis_index("ctx")
@@ -182,9 +193,12 @@
         pl.semaphore_signal(bar, inc=1, device_id=(flip(c, m), z), device_id_type=MESH)
     for device in planes:
         pl.semaphore_signal(bar, inc=1, device_id=device, device_id_type=MESH)
-    x_copy = local(0, x_hbm, x_v)
-    og_copy = local(1, og_hbm, og_v)
-    sa[pl.ds(pl.multiple_of(c * J, 8), J)] = seg_ref[...]
+    own_seg = sa.at[pl.ds(pl.multiple_of(c * J, 8), J)]
+    w_copies = [local(n, *pair) for n, pair in enumerate(((wi_hbm, wi_ref), (wc_hbm, wc_ref), (wo_hbm, wo_ref)))]
+    vec_copies = [local(3 + n, *pair) for n, pair in enumerate(zip(vec_hbm, vec_refs))]
+    seg_copy = local(12, seg_hbm, own_seg)
+    x_copy = local(13, x_hbm, x_v)
+    og_copy = local(14, og_hbm, og_v)
 
     def pack(name, take, put, copies_of, dtype):
         form, base = forms[name], bases[name]
@@ -229,26 +243,32 @@
         share = forms[name].size // 2
         return pl.ds(pl.multiple_of(bases[name] + which * share, 16), share)
 
+    others = half_chips - 1
+
     def z_send(name):
-        rows = part(name, slot_in_order)
-        return [copies.start(wps.at[0, rows], wps.at[d + 1, rows], planes[d]) for d in range(W - 1)]
+        rows = half(name, k) if name in cfg["z_only"] else part(name, slot_in_order)
+        moves = [(wps.at[0, rows], wps.at[d + 1, rows], planes[d]) for d in range(W - 1)]
+        return copies.start(moves, wps.at[pl.ds(1, W - 1), rows])
 
     def plane_send(name, before):
-        for copy in before:
-            copy.wait_recv()
+        if name in cfg["z_only"]:
+            return before
+        before.wait()
         there = wps.at[pl.ds(1, W - 1), part(name, slot_in_order)]
-        return [copies.start(there, there, device) for device in chips]
+        size = wps.at[pl.ds(1, W - 1), pl.ds(bases[name], others * (forms[name].size // C))]
+        return copies.start([(there, there, device) for device in chips], size)
 
     def sibling_send(name, before):
-        for copy in before:
-            copy.wait_recv()
+        before.wait()
         there = wps.at[pl.ds(1, W - 1), half(name, k)]
-        return copies.start(there, there, sibling)
-
+        return copies.start([(there, there, sibling)], there)
+
+    w_copies[0].wait()
     w_in[:, 0:width] = wi_ref[...].T
     pack("in", own_shard["in"], put_own, (0,), BF16)
     rows = []
-    for ref in vec_refs:
+    for ref, copy in zip(vec_refs, vec_copies):
+        copy.wait()
         row = ref[...].astype(F32).reshape(1, ref.shape[0])
         for h in range(ref.shape[0] // width):
             rows.append(
@@ -257,35 +277,43 @@
     rows.append(jnp.zeros((16 - len(rows), LANES), F32))
     vecb[0] = jnp.concatenate(rows, axis=0).astype(BF16)
     pl.semaphore_wait(bar, C - 1 + W - 1)
-    vec_sends = [copies.start(vecb.at[0], vecb.at[d + 1], planes[d]) for d in range(W - 1)]
+    vec_sends = copies.start(
+        [(vecb.at[0], vecb.at[d + 1], planes[d]) for d in range(W - 1)], vecb.at[pl.ds(1, W - 1)]
+    )
     w_z = {"in": z_send("in")}
-    for name in ("conv", "out"):
+    for name, copy in (("conv", w_copies[1]), ("out", w_copies[2])):
+        copy.wait()
         pack(name, own_shard[name], put_own, (0,), BF16)
         w_z[name] = z_send(name)
-    own_seg = sa.at[pl.ds(pl.multiple_of(c * J, 8), J)]
-    seg_sends = [copies.start(own_seg, own_seg, (flip(c, m), z)) for m in range(1, C)]
+    seg_copy.wait()
+    seg_sends = copies.start(
+        [(own_seg, own_seg, (flip(c, m), z)) for m in range(1, C)], sa.at[pl.ds(0, (C - 1) * J)]
+    )
     acc8[...] = jnp.zeros_like(acc8)
     acc4[...] = jnp.zeros_like(acc4)
+    a1[D : D + 16] = jnp.ones((16, R), BF16)
+    a3[H : H + 16] = jnp.ones((16, R), BF16)
+    bb[TAPS * H : TAPS * H + 16] = jnp.ones((16, R), BF16)
     vx[...] = jnp.zeros_like(vx)
 
-    def unpack(name, target, stacked=False):
+    def unpack(name, target):
         form, base = forms[name], bases[name]
         for start, count, panels in form.plain_spans():
             size = chunk_of(count)
-            groups = [[panel] for panel in panels] if stacked else [panels]
-            for g, group in enumerate(groups):
-
-                def step(i, first=g * form.rows + start, group=group, size=size):
-                    shift = i * size
-                    parts = [
-                        wps[flip(z, s), pl.ds(pl.multiple_of(base + row + shift, 16), size), lane : lane + columns]
-                        for s in shards
-                        for panel in group
-                        for row, lane, columns in panel
-                    ]
-                    target[pl.ds(pl.multiple_of(first + shift, 16), size), :] = jnp.concatenate(parts, axis=1)
-
-                loop(count // size, step)
+            order = [(s, panel) for s in shards for panel in panels]
+            if name == "conv":
+                order = [(s, panel) for panel in panels for s in shards]
+
+            def step(i, start=start, order=order, size=size):
+                shift = i * size
+                parts = [
+                    wps[flip(z, s), pl.ds(pl.multiple_of(base + row + shift, 16), size), lane : lane + columns]
+                    for s, panel in order
+                    for row, lane, columns in panel
+                ]
+                target[pl.ds(pl.multiple_of(start + shift, 16), size), :] = jnp.concatenate(parts, axis=1)
+
+            loop(count // size, step)
 
     def lanes_at(start):
         return pl.ds(pl.multiple_of(start, LG), LG)
@@ -294,14 +322,12 @@
         return [slice(f, f + FB) for f in range(0, n, FB)]
 
     x_copy.wait()
-    og_copy.wait()
 
     def first_stats(i):
         lanes = lanes_at(i * LG)
         acc = jnp.zeros((8, LG), F32)
         for f in blocks(D):
             acc += fold_rows(x_v[f, lanes].astype(F32))
-            acc8[2, f] += fold_lanes(og_v[f, lanes].astype(F32))
         mean = total_rows(acc) * (1.0 / D)
         acc = jnp.zeros((8, LG), F32)
         for f in blocks(D):
@@ -312,8 +338,7 @@
 
     loop(R // LG, first_stats)
 
-    for copy in vec_sends:
-        copy.wait_recv()
+    vec_sends.wait()
     vecs = [vecb[flip(z, s)].astype(F32) for s in shards]
     narrow = jnp.concatenate([v[:, :width] for v in vecs], axis=1).T
     for i in range(6):
@@ -340,18 +365,16 @@
             a1[f, lanes] = (pre * jnp.tanh(pre) + pre).astype(BF16)
 
     w_plane = {"in": plane_send("in", w_z["in"])}
-    loop(R // LG // 2, first_act)
+    loop(R // LG, first_act)
+    w_sib = {"in": sibling_send("in", w_plane["in"])}
     w_plane["conv"] = plane_send("conv", w_z["conv"])
-    loop(R // LG // 2, lambda i: first_act(i + R // LG // 2))
-    w_plane["out"] = plane_send("out", w_z["out"])
-    w_sib = {"in": sibling_send("in", w_plane["in"])}
-    w_sib["in"].wait_recv()
+    w_sib["in"].wait()
     unpack("in", w_in)
     w_inT[...] = w_in[...].T
 
     def second(chunk):
         here = slice(chunk * CW, (chunk + 1) * CW)
-        h2[:, here] = dot(w_inT[...], a1[:, here])
+        h2[:, here] = dot(w_inT[...], a1[0:D, here])
 
         def step(i):
             lanes = lanes_at(chunk * CW + i * LG)
@@ -371,26 +394,23 @@
             for f in blocks(H):
                 normed = (h2[f, lanes] - mean) * scaled
                 pre = normed * dup(p4[0, f], LG) + dup(p4[1, f], LG)
-                a2[f, lanes] = (pre * jnp.tanh(pre) + pre).astype(BF16)
+                bb[f, lanes] = (pre * jnp.tanh(pre) + pre).astype(BF16)
 
         loop(CW // LG, step)
 
     def edge_send(store, source, chunk, first):
         lanes = slice(chunk * EW, (chunk + 1) * EW)
-        store[c, :, lanes] = jnp.concatenate(
-            [source[:, j * BLK + first : j * BLK + first + EDGE] for j in range(chunk * CJ, (chunk + 1) * CJ)], axis=1
+        store[k, p, :, lanes] = jnp.concatenate(
+            [source[0:H, j * BLK + first : j * BLK + first + EDGE] for j in range(chunk * CJ, (chunk + 1) * CJ)],
+            axis=1,
         )
-        there = store.at[c, :, lanes]
-        return [copies.start(there, there, device) for device in chips], copies.start(there, there, sibling)
-
-    def edge_forward(store, sends, chunk):
-        lanes = slice(chunk * EW, (chunk + 1) * EW)
-        passed = []
-        for e in range(1, half_chips):
-            there = store.at[flip(c, 2 * e), :, lanes]
-            sends[e - 1].wait_recv()
-            passed.append(copies.start(there, there, sibling))
-        return passed
+        there = store.at[k, p, :, lanes]
+        return copies.start([(there, there, device) for device in chips], store.at[k, pl.ds(0, others), :, lanes])
+
+    def edge_forward(store, before, chunk):
+        before.wait()
+        there = store.at[k, :, :, slice(chunk * EW, (chunk + 1) * EW)]
+        return copies.start([(there, there, sibling)], there)
 
     mine = [deal[c * J + j] for j in range(J)]
     edge_lane = lax.broadcasted_iota(jnp.int32, (1, J * EDGE), 1)
@@ -408,15 +428,13 @@
     )
 
     def edge_take(store, waits, step, target):
-        for copy in waits:
-            copy.wait_recv()
+        for group in waits:
+            group.wait()
         wanted = edge_block + step
         total = jnp.zeros((H, J * EDGE), F32)
         for device in range(C):
-            chosen = [
-                diagonal * jnp.where(wanted == deal[device * J + j], 1.0, 0.0) for j in range(J)
-            ]
-            total += dot(store[device], jnp.concatenate(chosen, axis=0).astype(BF16))
+            chosen = [diagonal * jnp.where(wanted == deal[device * J + j], 1.0, 0.0) for j in range(J)]
+            total += dot(store[device % 2, device // 2], jnp.concatenate(chosen, axis=0).astype(BF16))
         target[...] = total.astype(BF16)
 
     def seg_take(step):
@@ -426,17 +444,15 @@
             out = jnp.where(wanted == deal[slot], jnp.broadcast_to(sa[slot : slot + 1], (J, BLK)), out)
         return out
 
-    t_first, t_near, t_passed = [], [], []
+    t_first, t_passed = [], []
     for chunk in range(CHUNKS):
         second(chunk)
-        sends, near = edge_send(ta, a2, chunk, BLK - EDGE)
-        t_first.append(sends)
-        t_near.append(near)
+        t_first.append(edge_send(ta, bb, chunk, BLK - EDGE))
     w_sib["conv"] = sibling_send("conv", w_plane["conv"])
+    w_plane["out"] = plane_send("out", w_z["out"])
     w_sib["out"] = sibling_send("out", w_plane["out"])
 
-    for copy in seg_sends:
-        copy.wait_recv()
+    seg_sends.wait()
     own, before, behind = sa[pl.ds(pl.multiple_of(c * J, 8), J)], seg_take(-1), seg_take(1)
     cut = BLK - STEP
 
@@ -454,27 +470,27 @@
     def tall(mask):
         return jnp.concatenate([mask] * (H // 16), axis=0)
 
-    w_sib["conv"].wait_recv()
-    unpack("conv", w_cv, stacked=True)
-    for tap in range(TAPS):
-        w_cvT[tap] = w_cv[tap * H : (tap + 1) * H].T
-    w_sib["out"].wait_recv()
+    w_sib["conv"].wait()
+    unpack("conv", w_cv)
+    w_cvT[:, 0 : TAPS * H] = jnp.concatenate([w_cv[:, tap * H : (tap + 1) * H].T for tap in range(TAPS)], axis=1)
+    w_sib["out"].wait()
     unpack("out", w_out)
     for chunk in range(CHUNKS):
-        t_passed += edge_forward(ta, t_first[chunk], chunk)
+        t_passed.append(edge_forward(ta, t_first[chunk], chunk))
+    og_copy.wait()
     for chunk in range(CHUNKS):
         here = slice(chunk * CW, (chunk + 1) * CW)
         g3[:, here] = dot(w_out[...], og_v[:, here])
-    edge_take(ta, t_near + t_passed, -1, pt)
+    edge_take(ta, t_passed, -1, pt)
 
     def third(chunk):
         here = slice(chunk * CW, (chunk + 1) * CW)
         for j in range(chunk * CJ, (chunk + 1) * CJ):
             tile, edge = slice(j * BLK, (j + 1) * BLK), slice(j * EDGE, (j + 1) * EDGE)
-            own, prev = a2[:, tile], pt[:, edge]
-            b1[:, tile] = jnp.concatenate([prev[:, STEP:], own[:, :cut]], axis=1) * tall(m1[:, tile])
-            b2[:, tile] = jnp.concatenate([prev, own[:, : BLK - EDGE]], axis=1) * tall(m2[:, tile])
-        c3[:, here] = dot(w_cvT[0], a2[:, here]) + dot(w_cvT[1], b1[:, here]) + dot(w_cvT[2], b2[:, here])
+            own, prev = bb[0:H, tile], pt[:, edge]
+            bb[H : 2 * H, tile] = jnp.concatenate([prev[:, STEP:], own[:, :cut]], axis=1) * tall(m1[:, tile])
+            bb[2 * H : 3 * H, tile] = jnp.concatenate([prev, own[:, : BLK - EDGE]], axis=1) * tall(m2[:, tile])
+        c3[:, here] = dot(w_cvT[:, 0 : TAPS * H], bb[0 : TAPS * H, here])
 
         def step(i):
             lanes = lanes_at(chunk * CW + i * LG)
@@ -508,16 +524,13 @@
                 normed = (c3[f, lanes] - mean) * scaled
                 grad = (scaled * (g3[f, lanes] - first - normed * second)).astype(BF16)
                 gv[f, lanes] = grad
-                acc4[5, f] += fold_lanes(grad.astype(F32))
 
         loop(CW // LG, step)
 
-    h_first, h_near, h_passed = [], [], []
+    h_first, h_passed = [], []
     for chunk in range(CHUNKS):
         third(chunk)
-        sends, near = edge_send(ha, gv, chunk, 0)
-        h_first.append(sends)
-        h_near.append(near)
+        h_first.append(edge_send(ha, gv, chunk, 0))
 
     taps_at = (c3, g3, big)
     whole_grad = {
@@ -538,15 +551,22 @@
     def shared(name):
         return pl.ds(bases[name] // C, forms[name].size // C)
 
-    def reduce_1(name):
-        return copies.start(psg.at[:, half(name, 1 - k)], rx1.at[:, halved(name)], sibling)
+    def keep_row(index, row):
+        at, count = vec_at[index][1], row.shape[1]
+        for t in range(-(-count // LANES)):
+            size = min(LANES, count - t * LANES)
+            vx[at + t : at + t + 1, 0:size] = row[:, t * LANES : t * LANES + size]
 
     def tiles(rows, body):
         size = chunk_of(rows)
         loop(rows // size, lambda i: body(pl.multiple_of(i * size, 16), size))
 
-    def reduce_2(name, before):
-        before.wait_recv()
+    def reduce_1(name):
+        there = rx1.at[:, halved(name)]
+        return copies.start([(psg.at[:, half(name, 1 - k)], there, sibling)], there)
+
+    def add_sibling(name, before):
+        before.wait()
         form = forms[name]
         first, mine = bases[name] // 2, bases[name] + k * (form.size // 2)
 
@@ -557,16 +577,19 @@
                 psg[d, here] = (psg[d, here].astype(F32) + rx1[d, to].astype(F32)).astype(BF16)
 
         tiles(form.size // 2, add)
-        share = form.size // C
-        sends = []
+        return mine
+
+    def plane_2(name, before):
+        mine = add_sibling(name, before)
+        share = forms[name].size // C
+        moves = []
         for e, device in enumerate(chips):
             rows = pl.ds(pl.multiple_of(mine + flip(p, e + 1) * share, 16), share)
-            sends.append(copies.start(psg.at[:, rows], rx2.at[e, :, shared(name)], device))
-        return sends
-
-    def reduce_3(name, before):
-        for copy in before:
-            copy.wait_recv()
+            moves.append((psg.at[:, rows], rx2.at[e, :, shared(name)], device))
+        return copies.start(moves, rx2.at[:, :, shared(name)])
+
+    def plane_3(name, before):
+        before.wait()
         share = forms[name].size // C
         first, mine = bases[name] // C, bases[name] + slot_in_order * share
 
@@ -575,16 +598,16 @@
             here = pl.ds(pl.multiple_of(mine + at, 16), size)
             for d in range(W):
                 total = psg[d, here].astype(F32)
-                for e in range(half_chips - 1):
+                for e in range(others):
                     total = total + rx2[e, d, to].astype(F32)
                 s2[d, to] = total.astype(BF16)
 
         tiles(share, add)
-        return [copies.start(s2.at[d + 1, shared(name)], rx3.at[d, shared(name)], planes[d]) for d in range(W - 1)]
-
-    def reduce_4(name, before):
-        for copy in before:
-            copy.wait_recv()
+        moves = [(s2.at[d + 1, shared(name)], rx3.at[d, shared(name)], planes[d]) for d in range(W - 1)]
+        return copies.start(moves, rx3.at[:, shared(name)])
+
+    def plane_4(name, before):
+        before.wait()
         share = forms[name].size // C
         first, mine = bases[name] // C, bases[name] + slot_in_order * share
 
@@ -593,30 +616,85 @@
             total = s2[0, to].astype(F32)
             for d in range(W - 1):
                 total = total + rx3[d, to].astype(F32)
-            fo[pl.ds(pl.multiple_of(mine + at, 16), size)] = total
+            fo[pl.ds(pl.multiple_of(mine + at, 16), size)] = total.astype(BF16)
 
         tiles(share, add)
         there = fo.at[part(name, slot_in_order)]
-        return [copies.start(there, there, device) for device in chips]
-
-    def reduce_5(name, before):
-        for copy in before:
-            copy.wait_recv()
+        return copies.start([(there, there, device) for device in chips], fo.at[pl.ds(bases[name], others * share)])
+
+    def plane_5(name, before):
+        before.wait()
         there = fo.at[half(name, k)]
-        return copies.start(there, there, sibling)
-
-    big[0:H, 0:D] = dot(a3[...], og_v[...], (1, 1))
+        return copies.start([(there, there, sibling)], there)
+
+    def column_2(name, before):
+        add_sibling(name, before)
+        there = pl.ds(cfg["rz_at"][name], forms[name].size // 2)
+        moves = [(psg.at[d + 1, half(name, k)], rz.at[d, there], planes[d]) for d in range(W - 1)]
+        return copies.start(moves, rz.at[:, there])
+
+    def column_3(name, before):
+        before.wait()
+        size_half, base = forms[name].size // 2, cfg["rz_at"][name]
+        mine = bases[name] + k * size_half
+
+        def add(at, size):
+            total = psg[0, pl.ds(pl.multiple_of(mine + at, 16), size)].astype(F32)
+            to = pl.ds(pl.multiple_of(base + at, 16), size)
+            for d in range(W - 1):
+                total = total + rz[d, to].astype(F32)
+            tz[p, to] = total.astype(BF16)
+
+        tiles(size_half, add)
+        there = tz.at[p, pl.ds(base, size_half)]
+        return copies.start(
+            [(there, there, device) for device in chips], tz.at[pl.ds(0, others), pl.ds(base, size_half)]
+        )
+
+    def column_4(name, before):
+        before.wait()
+        size_half, base = forms[name].size // 2, cfg["rz_at"][name]
+        mine = bases[name] + k * size_half
+
+        def add(at, size):
+            to = pl.ds(pl.multiple_of(base + at, 16), size)
+            total = tz[0, to].astype(F32)
+            for chip in range(1, half_chips):
+                total = total + tz[chip, to].astype(F32)
+            fo[pl.ds(pl.multiple_of(mine + at, 16), size)] = total.astype(BF16)
+
+        tiles(size_half, add)
+        there = fo.at[half(name, k)]
+        return copies.start([(there, there, sibling)], there)
+
+    def same_group(name, before):
+        return before
+
+    steps = {}
+    for name in forms:
+        first = cfg["z_first"]
+        steps[name] = (column_2, column_3, column_4, same_group) if name in first else (plane_2, plane_3, plane_4, plane_5)
+    going = {}
+
+    def reduce(name, step):
+        going[name] = reduce_1(name) if step == 1 else steps[name][step - 2](name, going[name])
+
+    big[0 : H + 16, 0:D] = dot(a3[...], og_v[...], (1, 1))
+    keep_row(2, big[H : H + 1, 0:D])
     pack_grad("out")
-    g_out = reduce_1("out")
-    for tap, source in enumerate((a2, b1, b2)):
-        taps_at[tap][0:H, 0:H] = dot(source[...], gv[...], (1, 1))
+    reduce("out", 1)
+    for tap in range(TAPS):
+        rows = H + 16 if tap == TAPS - 1 else H
+        value = dot(bb[tap * H : tap * H + rows], gv[...], (1, 1))
+        taps_at[tap][0:H, 0:H] = value[0:H]
+    keep_row(8, value[H : H + 1])
+    reduce("out", 2)
     pack_grad("conv")
-    g_conv = reduce_1("conv")
+    reduce("conv", 1)
     for chunk in range(CHUNKS):
-        h_passed += edge_forward(ha, h_first[chunk], chunk)
-    g_out = reduce_2("out", g_out)
-    g_conv = reduce_2("conv", g_conv)
-    edge_take(ha, h_near + h_passed, 1, nh)
+        h_passed.append(edge_forward(ha, h_first[chunk], chunk))
+    reduce("conv", 2)
+    edge_take(ha, h_passed, 1, nh)
 
     def second_back(chunk):
         here = slice(chunk * CW, (chunk + 1) * CW)
@@ -624,12 +702,11 @@
             tile, edge = slice(j * BLK, (j + 1) * BLK), slice(j * EDGE, (j + 1) * EDGE)
             own, late = gv[:, tile], nh[:, edge]
             shifted = (late * tall(k1[:, edge]))[:, :STEP]
-            b1[:, tile] = jnp.concatenate([(own * tall(m1[:, tile]))[:, STEP:], shifted], axis=1)
+            bb[0:H, tile] = own
+            bb[H : 2 * H, tile] = jnp.concatenate([(own * tall(m1[:, tile]))[:, STEP:], shifted], axis=1)
             shifted = late * tall(k2[:, edge])
-            b2[:, tile] = jnp.concatenate([(own * tall(m2[:, tile]))[:, EDGE:], shifted], axis=1)
-        c3[:, here] = (
-            dot(w_cv[0:H], gv[:, here]) + dot(w_cv[H : 2 * H], b1[:, here]) + dot(w_cv[2 * H : 3 * H], b2[:, here])
-        )
+            bb[2 * H : 3 * H, tile] = jnp.concatenate([(own * tall(m2[:, tile]))[:, EDGE:], shifted], axis=1)
+        c3[:, here] = dot(w_cv[...], bb[0 : TAPS * H, here])
 
         def step(i):
             lanes = lanes_at(chunk * CW + i * LG)
@@ -652,22 +729,52 @@
                 normed = (h2[f, lanes] - mean) * scaled
                 grad = (scaled * (c3[f, lanes] - first - normed * second)).astype(BF16)
                 gh[f, lanes] = grad
-                acc4[4, f] += fold_lanes(grad.astype(F32))
 
         loop(CW // LG, step)
 
-    for chunk in range(CHUNKS):
-        second_back(chunk)
-    big[:, 0:H] = dot(a1[...], gh[...], (1, 1))
+    second_back(0)
+    second_back(1)
+    reduce("out", 3)
+    big[0 : D + 16, 0:H] = dot(a1[...], gh[...], (1, 1))
+    keep_row(7, big[D : D + 1, 0:H])
     pack_grad("in")
-    g_in = reduce_1("in")
-    g_out = reduce_3("out", g_out)
+    reduce("in", 1)
+
+    def sums_rows(indices):
+        for index in indices:
+            (group, i, _, scale), _ = vec_at[index]
+            keep_row(index, jnp.sum((acc8 if group == 8 else acc4)[i].T, 0, keepdims=True) * scale)
+
+    def sums_plane(rows):
+        vr[c, rows] = vx[rows]
+        there = vr.at[c, rows]
+        return copies.start([(there, there, (flip(c, m), z)) for m in range(1, C)], vr.at[pl.ds(0, C - 1), rows])
+
+    def sums_column(rows, before):
+        before.wait()
+        total = vr[0, rows]
+        for m in range(1, C):
+            total = total + vr[m, rows]
+        vs[rows] = total
+        return copies.start([(vs.at[rows], vz.at[d, rows], planes[d]) for d in range(W - 1)], vz.at[:, rows])
+
+    def sums_end(rows, before):
+        before.wait()
+        total = vs[rows]
+        for d in range(W - 1):
+            total = total + vz[d, rows]
+        vo_ref[rows] = total
+
+    late, early = slice(0, cfg["v_late"]), slice(cfg["v_late"], cfg["v_rows"])
+    sums_rows((3, 4, 5, 6))
+    v_early = sums_plane(early)
+    reduce("conv", 3)
     for side in range(D // H):
-        w_cvT[side] = w_out[:, side * H : (side + 1) * H].T
+        w_cvT[:, side * 512 : side * 512 + H] = w_out[:, side * H : (side + 1) * H].T
 
     def first_back(chunk):
         here = slice(chunk * CW, (chunk + 1) * CW)
-        big[:, here] = dot(w_in[...], gh[:, here])
+        big[0:D, here] = dot(w_in[...], gh[:, here])
 
         def step(i):
             lanes = lanes_at(chunk * CW + i * LG)
@@ -692,12 +799,12 @@
                 big[f, lanes] = og_v[f, lanes].astype(F32) + grad
 
         loop(CW // LG, step)
-        return local(2 + chunk, big.at[:, here], ig_hbm.at[:, here])
+        return local(chunk, big.at[0:D, here], ig_hbm.at[:, here])
 
     def last(chunk):
         here = slice(chunk * CW, (chunk + 1) * CW)
         for side, store in enumerate((c3, g3)):
-            store[:, 0:CW] = dot(w_cvT[side], a3[:, here])
+            store[:, 0:CW] = dot(w_cvT[:, side * 512 : side * 512 + H], a3[0:H, here])
 
             def step(i, side=side, store=store):
                 lanes, at = lanes_at(chunk * CW + i * LG), lanes_at(i * LG)
@@ -707,50 +814,35 @@
                     x_v[to, lanes] = (x_v[to, lanes].astype(F32) + value).astype(BF16)
 
             loop(CW // LG, step)
-        return local(4 + chunk, x_v.at[:, here], bo_hbm.at[:, here])
+        return local(2 + chunk, x_v.at[:, here], bo_hbm.at[:, here])
+
+    def leave(n, name):
+        rows = pl.ds(bases[name], forms[name].size)
+        going[name].wait()
+        return local(n, fo.at[rows], fo_hbm.at[rows])
 
     out_copies = [first_back(0)]
-    g_in = reduce_2("in", g_in)
-    g_conv = reduce_3("conv", g_conv)
+    reduce("in", 2)
     out_copies.append(first_back(1))
-
-    def row_sums(group, i, scale):
-        return jnp.sum((acc8 if group == 8 else acc4)[i].T, 0, keepdims=True) * scale
-
-    for (group, i, count, scale), at in vec_at:
-        value = row_sums(group, i, scale)
-        for t in range(-(-count // LANES)):
-            size = min(LANES, count - t * LANES)
-            vx[at + t : at + t + 1, 0:size] = value[:, t * LANES : t * LANES + size]
-    vr[c] = vx[...]
-    v_sends = [copies.start(vr.at[c], vr.at[c], (flip(c, m), z)) for m in range(1, C)]
-    g_in = reduce_3("in", g_in)
-    g_out = reduce_4("out", g_out)
-    g_conv = reduce_4("conv", g_conv)
+    sums_rows((0, 1))
+    v_late = sums_plane(late)
+    v_early = sums_column(early, v_early)
+    reduce("in", 3)
+    reduce("conv", 4)
     out_copies.append(last(0))
-    for copy in v_sends:
-        copy.wait_recv()
-    total = vr[0]
-    for m in range(1, C):
-        total = total + vr[m]
-    vs[...] = total
-    z_sends = [copies.start(vs, vz.at[d], planes[d]) for d in range(W - 1)]
-    g_in = reduce_4("in", g_in)
+    v_late = sums_column(late, v_late)
+    reduce("out", 4)
     out_copies.append(last(1))
-    g_out = reduce_5("out", g_out)
-    g_conv = reduce_5("conv", g_conv)
-    g_in = reduce_5("in", g_in)
-    for copy in z_sends:
-        copy.wait_recv()
-    total = vs[...]
-    for d in range(W - 1):
-        total = total + vz[d]
-    vo_ref[...] = total
-    for copy in (g_out, g_conv, g_in):
-        copy.wait_recv()
-    out_copies.append(local(0, fo, fo_hbm))
-    for copy in copies.open:
-        copy.wait_send()
+    reduce("in", 4)
+    reduce("conv", 5)
+    out_copies.append(leave(4, "out"))
+    sums_end(early, v_early)
+    out_copies.append(leave(5, "conv"))
+    reduce("in", 5)
+    sums_end(late, v_late)
+    out_copies.append(leave(6, "in"))
+    for group in copies.groups:
+        group.wait_sent()
     for copy in out_copies:
         copy.wait()
 
@@ -797,7 +889,10 @@
         form, base, parts = forms[name], bases[name], []
         for start, count, panels in form.plain_spans():
             values = [
-                [fo[base + row : base + row + count, lane : lane + columns] for row, lane, columns in panel]
+                [
+                    fo[base + row : base + row + count, lane : lane + columns].astype(F32)
+                    for row, lane, columns in panel
+                ]
                 for panel in panels
             ]
             if name == "conv":
@@ -836,39 +931,44 @@
         bases[name] = total
         total += form.size
 
+    items = [(8, 0, D, 0.5), (8, 1, D, 0.5), (None, 0, D, 1.0)]
+    items += [(4, i, H, 0.5) if i < 4 else (None, 0, H, 1.0) for i in range(6)]
     vec_at, at = [], 0
-    for item in [(8, 0, D, 0.5), (8, 1, D, 0.5), (8, 2, D, 1.0)] + [
-        (4, i, H, 0.5 if i < 4 else 1.0) for i in range(6)
-    ]:
+    for n, item in enumerate(items):
+        if n == 2:
+            at = v_late = up(at, 8)
         vec_at.append((item, at))
         at += -(-item[2] // LANES)
     v_rows = up(at, 8)
     cfg = {
         "C": C, "W": W, "J": J, "D": D, "H": H, "forms": forms, "bases": bases, "width": width, "vec_at": vec_at,
     }
+    cfg["z_first"] = ("out",) if C <= 8 else ()
+    cfg["z_only"] = ("out",)
+    cfg["v_late"], cfg["v_rows"] = v_late, v_rows
+    cfg["rz_at"], rz_rows = {}, 0
+    for name in cfg["z_first"]:
+        cfg["rz_at"][name] = rz_rows
+        rz_rows += forms[name].size // 2
+    rz_rows = max(rz_rows, 16)
     R = rows
     others = max(C // 2 - 1, 1)
-    n_copies = (
-        3 * ((W - 1) + (C // 2 - 1) + 1) + (W - 1) + (C - 1) + 2 * CHUNKS * (2 * (C // 2 - 1) + 1)
-        + 3 * (2 * (C // 2 - 1) + (W - 1) + 2) + (C - 1) + (W - 1)
-    )
+    n_groups = 3 * 3 + 2 + 2 * 2 * CHUNKS + 3 * 5 + 4
     vmem = pltpu.VMEM
     scratch = [
         vmem((D, R), BF16),
         vmem((D, R), BF16),
         vmem((1, R), F32),
         vmem((1, R), F32),
-        vmem((D, R), BF16),
+        vmem((D + 16, R), BF16),
         vmem((H, R), F32),
         vmem((1, R), F32),
         vmem((1, R), F32),
+        vmem((TAPS * H + 16, R), BF16),
+        vmem((H + 16, R), BF16),
         vmem((H, R), BF16),
         vmem((H, R), BF16),
-        vmem((H, R), BF16),
-        vmem((H, R), BF16),
-        vmem((H, R), BF16),
-        vmem((H, R), BF16),
-        vmem((D, R), F32),
+        vmem((D + 16, R), F32),
         vmem((H, R), F32),
         vmem((H, R), F32),
         vmem((16, R), BF16),
@@ -877,14 +977,14 @@
         vmem((16, J * EDGE), BF16),
         vmem((D, H), BF16),
         vmem((H, D), BF16),
-        vmem((TAPS * H, H), BF16),
-        vmem((TAPS, H, H), BF16),
+        vmem((H, TAPS * H), BF16),
+        vmem((H, max(up(TAPS * H, LANES), 512 * (D // H))), BF16),
         vmem((H, D), BF16),
         vmem((W, total, LANES), BF16),
         vmem((W, 16, LANES), BF16),
         vmem((J * C, BLK), jnp.int32),
-        vmem((C, H, J * EDGE), BF16),
-        vmem((C, H, J * EDGE), BF16),
+        vmem((2, C // 2, H, J * EDGE), BF16),
+        vmem((2, C // 2, H, J * EDGE), BF16),
         vmem((H, J * EDGE), BF16),
         vmem((H, J * EDGE), BF16),
         vmem((W, total, LANES), BF16),
@@ -892,18 +992,24 @@
         vmem((others, W, total // C, LANES), BF16),
         vmem((W, total // C, LANES), BF16),
         vmem((W - 1, total // C, LANES), BF16),
-        vmem((total, LANES), F32),
+        vmem((W - 1, rz_rows, LANES), BF16),
+        vmem((C // 2 if cfg["z_first"] else 1, rz_rows, LANES), BF16),
+        vmem((total, LANES), BF16),
         vmem((3, D, LANES), F32),
         vmem((6, H, LANES), F32),
-        vmem((3, D, LANES), F32),
-        vmem((6, H, LANES), F32),
+        vmem((2, D, LANES), F32),
+        vmem((4, H, LANES), F32),
         vmem((v_rows, LANES), F32),
         vmem((C, v_rows, LANES), F32),
         vmem((v_rows, LANES), F32),
         vmem((W - 1, v_rows, LANES), F32),
-        pltpu.SemaphoreType.DMA((6,)),
-        pltpu.SemaphoreType.DMA((n_copies,)),
-        pltpu.SemaphoreType.DMA((n_copies,)),
+        vmem((width, D), BF16),
+        vmem((TAPS, H, width), BF16),
+        vmem((H, panels * width), BF16),
+        *[vmem((n // W,), BF16) for n in (D, D, H, H, H, H, H, H, D)],
+        pltpu.SemaphoreType.DMA((15,)),
+        pltpu.SemaphoreType.DMA((n_groups,)),
+        pltpu.SemaphoreType.DMA((n_groups,)),
     ]
     any_spec = pl.BlockSpec(memory_space=pl.ANY)
     vmem_spec = pl.BlockSpec(memory_space=pltpu.VMEM)
@@ -918,10 +1024,10 @@
         out_shape=(
             jax.ShapeDtypeStruct((D, R), BF16),
             jax.ShapeDtypeStruct((D, R), F32),
-            jax.ShapeDtypeStruct((total, LANES), F32),
+            jax.ShapeDtypeStruct((total, LANES), BF16),
             jax.ShapeDtypeStruct((v_rows, LANES), F32),
         ),
-        in_specs=[pl.BlockSpec(memory_space=pltpu.SMEM), any_spec, any_spec] + [vmem_spec] * 13,
+        in_specs=[pl.BlockSpec(memory_space=pltpu.SMEM)] + [any_spec] * 15,
         out_specs=(any_spec, any_spec, any_spec, vmem_spec),
         scratch_shapes=flat,
         compiler_params=pltpu.CompilerParams(
@@ -954,7 +1060,7 @@
         in_specs=[any_spec, any_spec, any_spec, vmem_spec],
         out_specs=(any_spec,) * 5 + (vmem_spec,) * 9,
         scratch_shapes=[
-            vmem((D, R), F32), vmem((D, R), BF16), vmem((total, LANES), F32),
+            vmem((D, R), F32), vmem((D, R), BF16), vmem((total, LANES), BF16),
             vmem((width, D), F32), vmem((TAPS, H, width), F32), vmem((H, panels * width), F32),
             pltpu.SemaphoreType.DMA((4 * SPREAD + 4,)),
         ],

time: 86 us -> 79.8 us (0.928)
  Pallas kernels: 84.2 us -> 78.3 us
    pallas_call x1, Pallas kernels: 78.2 us -> 72.5 us  [on_device(): pl.pallas_call(run, out_shape=(jax.ShapeDtypeStruct((D, R), BF16), jax.Sh...]
where the time goes in v3:
time: 79.8 us; the launch traced here: 79.1 us
  Pallas kernels  78.3 us (98%)
  between operations  0.82 us (1%)
    pallas_call x1, Pallas kernels, on_device(): pl.pallas_call(run, out_shape=(jax.ShapeDtypeStruct((D, R), BF16), jax.Sh...  72.5 us
    pallas_call x1, Pallas kernels, on_device(): pl.pallas_call(lambda *refs: spread(cfg, *refs), out_shape=(jax.ShapeDtyp...  5.78 us

profile of v3, /device:TPU:0, one launch (start us, length us, event | category | flops | bytes accessed | tf_op | source)
XLA Modules:
  0.0 79.1 jit_solution(2221724212131386222)
XLA Ops:
  0.7 72.5 %block.1 = (bf16[800,1024]{1,0:T(8,128)(2,1)}, f32[800,1024]{1,0:T(8,128)}, bf16[2304,128]{1,0:T(8,128)(2,1)}, f32[48,128]{1,0:T(8,128)}) custom-call(s32[64]{0:T(128)} %refs_0_.1, bf16[800,1024]{1,0:T(8,128)(2,1)} %bitcast.16, bf16[800,1024]{1,0:T(8,128)(2,1)} %bitcast.17, s32[8,128]{1,0:T(8,128)} %bitcast.21, bf16[100,800]{1,0:T(8,128)(2,1)} %bitcast.20, ...), custom_call_target="tpu_custom_call" | custom-call | flops 6881280000 | bytes 8192000 | tf_op jit(solution)/shard_map/block/pallas_call | solution.py:1022
  73.1 5.8 %spread.1 = (bf16[800,1024]{1,0:T(8,128)(2,1)}, f32[800,1024]{1,0:T(8,128)}, f32[100,800]{1,0:T(8,128)}, f32[3,400,100]{2,1,0:T(8,128)}, f32[400,200]{1,0:T(8,12...) custom-call(bf16[800,1024]{1,0:T(8,128)(2,1)} %get-tuple-element.32., ...), custom_call_target="tpu_custom_call" | custom-call | bytes 11468800 | tf_op jit(solution)/shard_map/spread/pallas_call | solution.py:1050

commit v4 on v3

--- a/solution.py
+++ b/solution.py
@@ -161,13 +161,13 @@
     EW = CJ * EDGE
     (deal, x_hbm, og_hbm, seg_hbm, wi_hbm, wc_hbm, wo_hbm) = refs[:7]
     vec_hbm = refs[7:16]
-    (bo_hbm, ig_hbm, fo_hbm, vo_ref) = refs[16:20]
+    (bo_hbm, ig_hbm, fo_hbm, sm_hbm, vo_ref) = refs[16:21]
     (
         x_v, og_v, mu1, sc1, a1, h2, mu2, sc2, bb, a3, gv, gh, big, c3, g3,
         m1, m2, k1, k2, w_in, w_inT, w_cv, w_cvT, w_out, wps, vecb, sa, ta, ha, pt, nh,
         psg, rx1, rx2, s2, rx3, rz, tz, fo, p8, p4, acc8, acc4, vx, vr, vs, vz,
         wi_ref, wc_ref, wo_ref, *vec_refs, lsem, ssem, rsem,
-    ) = refs[20:]
+    ) = refs[21:]
 
     c = lax.axis_index("ctx")
     z = lax.axis_index("wsh")
@@ -235,13 +235,15 @@
         "conv": lambda s, panel, rows, columns: wc_ref[panel, rows, columns],
         "out": lambda s, panel, rows, columns: wo_ref[rows, moved(columns, width * panel)],
     }
+    spans = cfg["spans"]
+
     def part(name, order):
-        share = forms[name].size // C
-        return pl.ds(pl.multiple_of(bases[name] + order * share, 16), share)
+        base, size = spans[name]
+        return pl.ds(pl.multiple_of(base + order * (size // C), 16), size // C)
 
     def half(name, which):
-        share = forms[name].size // 2
-        return pl.ds(pl.multiple_of(bases[name] + which * share, 16), share)
+        base, size = spans[name]
+        return pl.ds(pl.multiple_of(base + which * (size // 2), 16), size // 2)
 
     others = half_chips - 1
 
@@ -255,7 +257,8 @@
             return before
         before.wait()
         there = wps.at[pl.ds(1, W - 1), part(name, slot_in_order)]
-        size = wps.at[pl.ds(1, W - 1), pl.ds(bases[name], others * (forms[name].size // C))]
+        base, size = spans[name]
+        size = wps.at[pl.ds(1, W - 1), pl.ds(base, others * (size // C))]
         return copies.start([(there, there, device) for device in chips], size)
 
     def sibling_send(name, before):
@@ -280,11 +283,12 @@
     vec_sends = copies.start(
         [(vecb.at[0], vecb.at[d + 1], planes[d]) for d in range(W - 1)], vecb.at[pl.ds(1, W - 1)]
     )
-    w_z = {"in": z_send("in")}
+    w_z = {name: z_send(name) for name in cfg["in_spans"]}
     for name, copy in (("conv", w_copies[1]), ("out", w_copies[2])):
         copy.wait()
         pack(name, own_shard[name], put_own, (0,), BF16)
-        w_z[name] = z_send(name)
+        if name == "conv":
+            w_z[name] = z_send(name)
     seg_copy.wait()
     seg_sends = copies.start(
         [(own_seg, own_seg, (flip(c, m), z)) for m in range(1, C)], sa.at[pl.ds(0, (C - 1) * J)]
@@ -364,11 +368,13 @@
             pre = normed * dup(p8[0, f], LG) + dup(p8[1, f], LG)
             a1[f, lanes] = (pre * jnp.tanh(pre) + pre).astype(BF16)
 
-    w_plane = {"in": plane_send("in", w_z["in"])}
+    w_plane = {name: plane_send(name, w_z[name]) for name in cfg["in_spans"]}
     loop(R // LG, first_act)
-    w_sib = {"in": sibling_send("in", w_plane["in"])}
+    w_sib = {name: sibling_send(name, w_plane[name]) for name in cfg["in_spans"]}
     w_plane["conv"] = plane_send("conv", w_z["conv"])
-    w_sib["in"].wait()
+    w_z["out"] = z_send("out")
+    for name in cfg["in_spans"]:
+        w_sib[name].wait()
     unpack("in", w_in)
     w_inT[...] = w_in[...].T
 
@@ -398,6 +404,9 @@
 
         loop(CW // LG, step)
 
+    relay = half_chips == 4
+    upper, lower = slice(0, H // 32 * 16), slice(H // 32 * 16, H)
+
     def edge_send(store, source, chunk, first):
         lanes = slice(chunk * EW, (chunk + 1) * EW)
         store[k, p, :, lanes] = jnp.concatenate(
@@ -405,12 +414,29 @@
             axis=1,
         )
         there = store.at[k, p, :, lanes]
-        return copies.start([(there, there, device) for device in chips], store.at[k, pl.ds(0, others), :, lanes])
+        if relay:
+            return [copies.start([(there, there, device)], there) for device in chips[:2]]
+        return [copies.start([(there, there, device) for device in chips], store.at[k, pl.ds(0, others), :, lanes])]
+
+    def edge_relay(store, before, chunk):
+        if not relay:
+            return before
+        lanes = slice(chunk * EW, (chunk + 1) * EW)
+        before[0].wait()
+        one = store.at[k, flip(p, 1), upper, lanes]
+        near = store.at[k, pl.ds(p // 2 * 2, 2), :, lanes]
+        first = copies.start([(one, one, chips[1])], one)
+        near = copies.start([(near, near, sibling)], near)
+        before[1].wait()
+        two = store.at[k, flip(p, 2), lower, lanes]
+        return [first, copies.start([(two, two, chips[0])], two), near]
 
     def edge_forward(store, before, chunk):
-        before.wait()
-        there = store.at[k, :, :, slice(chunk * EW, (chunk + 1) * EW)]
-        return copies.start([(there, there, sibling)], there)
+        lanes = slice(chunk * EW, (chunk + 1) * EW)
+        for group in before[:2]:
+            group.wait()
+        there = store.at[k, pl.ds(flip(p, 2) // 2 * 2, 2), :, lanes] if relay else store.at[k, :, :, lanes]
+        return before[2:] + [copies.start([(there, there, sibling)], there)]
 
     mine = [deal[c * J + j] for j in range(J)]
     edge_lane = lax.broadcasted_iota(jnp.int32, (1, J * EDGE), 1)
@@ -428,13 +454,18 @@
     )
 
     def edge_take(store, waits, step, target):
-        for group in waits:
+        wanted = edge_block + step
+
+        def choice(device):
+            chosen = [diagonal * jnp.where(wanted == deal[device * J + j], 1.0, 0.0) for j in range(J)]
+            return jnp.concatenate(chosen, axis=0).astype(BF16)
+
+        ready = [choice(device) for device in range(C)] if C <= 8 else None
+        for group in sum(waits, []):
             group.wait()
-        wanted = edge_block + step
         total = jnp.zeros((H, J * EDGE), F32)
         for device in range(C):
-            chosen = [diagonal * jnp.where(wanted == deal[device * J + j], 1.0, 0.0) for j in range(J)]
-            total += dot(store[device % 2, device // 2], jnp.concatenate(chosen, axis=0).astype(BF16))
+            total += dot(store[device % 2, device // 2], ready[device] if ready else choice(device))
         target[...] = total.astype(BF16)
 
     def seg_take(step):
@@ -472,15 +503,16 @@
 
     w_sib["conv"].wait()
     unpack("conv", w_cv)
+    t_first[0] = edge_relay(ta, t_first[0], 0)
     w_cvT[:, 0 : TAPS * H] = jnp.concatenate([w_cv[:, tap * H : (tap + 1) * H].T for tap in range(TAPS)], axis=1)
     w_sib["out"].wait()
     unpack("out", w_out)
-    for chunk in range(CHUNKS):
-        t_passed.append(edge_forward(ta, t_first[chunk], chunk))
+    t_first[1] = edge_relay(ta, t_first[1], 1)
     og_copy.wait()
     for chunk in range(CHUNKS):
         here = slice(chunk * CW, (chunk + 1) * CW)
         g3[:, here] = dot(w_out[...], og_v[:, here])
+        t_passed.append(edge_forward(ta, t_first[chunk], chunk))
     edge_take(ta, t_passed, -1, pt)
 
     def third(chunk):
@@ -620,9 +652,14 @@
 
         tiles(share, add)
         there = fo.at[part(name, slot_in_order)]
-        return copies.start([(there, there, device) for device in chips], fo.at[pl.ds(bases[name], others * share)])
+        devices = [(flip(c, m), z) for m in range(1, C)] if name in cfg["direct"] else chips
+        return copies.start(
+            [(there, there, device) for device in devices], fo.at[pl.ds(bases[name], len(devices) * share)]
+        )
 
     def plane_5(name, before):
+        if name in cfg["direct"]:
+            return before
         before.wait()
         there = fo.at[half(name, k)]
         return copies.start([(there, there, sibling)], there)
@@ -681,20 +718,22 @@
 
     big[0 : H + 16, 0:D] = dot(a3[...], og_v[...], (1, 1))
     keep_row(2, big[H : H + 1, 0:D])
+    h_first[0] = edge_relay(ha, h_first[0], 0)
     pack_grad("out")
     reduce("out", 1)
+    h_first[1] = edge_relay(ha, h_first[1], 1)
     for tap in range(TAPS):
         rows = H + 16 if tap == TAPS - 1 else H
         value = dot(bb[tap * H : tap * H + rows], gv[...], (1, 1))
         taps_at[tap][0:H, 0:H] = value[0:H]
     keep_row(8, value[H : H + 1])
     reduce("out", 2)
+    h_passed.append(edge_forward(ha, h_first[0], 0))
     pack_grad("conv")
     reduce("conv", 1)
-    for chunk in range(CHUNKS):
-        h_passed.append(edge_forward(ha, h_first[chunk], chunk))
+    h_passed.append(edge_forward(ha, h_first[1], 1))
+    edge_take(ha, h_passed, 1, nh)
     reduce("conv", 2)
-    edge_take(ha, h_passed, 1, nh)
 
     def second_back(chunk):
         here = slice(chunk * CW, (chunk + 1) * CW)
@@ -734,8 +773,8 @@
 
     second_back(0)
     second_back(1)
+    big[0 : D + 16, 0:H] = dot(a1[...], gh[...], (1, 1))
     reduce("out", 3)
-    big[0 : D + 16, 0:H] = dot(a1[...], gh[...], (1, 1))
     keep_row(7, big[D : D + 1, 0:H])
     pack_grad("in")
     reduce("in", 1)
@@ -817,9 +856,21 @@
         return local(2 + chunk, x_v.at[:, here], bo_hbm.at[:, here])
 
     def leave(n, name):
-        rows = pl.ds(bases[name], forms[name].size)
         going[name].wait()
-        return local(n, fo.at[rows], fo_hbm.at[rows])
+        form, base = forms[name], bases[name]
+        if name == "in":
+            rows = pl.ds(base, form.size)
+            return local(n, fo.at[rows], fo_hbm)
+        for start, count, panels in form.plain_spans():
+            values = [
+                [fo[base + row : base + row + count, lane : lane + columns].astype(F32) for row, lane, columns in panel]
+                for panel in panels
+            ]
+            for at, value in zip(cfg["small_at"][name], values if name == "conv" else [sum(values, [])]):
+                value = jnp.concatenate(value, axis=1)
+                h2[start : start + count, at : at + value.shape[1]] = value
+        first, last_lane = cfg["small_at"][name][0], cfg["small_end"][name]
+        return local(n, h2.at[:, first:last_lane], sm_hbm.at[:, first:last_lane])
 
     out_copies = [first_back(0)]
     reduce("in", 2)
@@ -849,8 +900,8 @@
 
 def spread(cfg, *refs):
     W, forms, bases, width, vec_at = (cfg[key] for key in ("W", "forms", "bases", "width", "vec_at"))
-    bo_in, ig_in, fo_in, vx, bo_out, ig_out, gi_out, gc_out, go_out = refs[:9]
-    vec_out, (ig_v, bo_v, fo, gi, gc, go, sem) = refs[9:18], refs[18:]
+    bo_in, ig_in, fo_in, sm_in, vx_in, bo_out, ig_out, gi_out, gc_out, go_out = refs[:10]
+    vec_out, (ig_v, bo_v, fo, sm, vx, gi, gc, go), vec_v, sem = refs[10:19], refs[19:27], refs[27:36], refs[36]
     z = lax.axis_index("wsh")
     used = 0
 
@@ -861,14 +912,14 @@
         move.start()
         return move
 
-    grads = copy(fo_in, fo)
-    pieces = []
+    early, pieces, moves = [], [], []
     for source, stage, target in ((ig_in, ig_v, ig_out), (bo_in, bo_v, bo_out)):
         size = source.shape[0] // SPREAD
         for i in range(SPREAD):
             rows = pl.ds(i * size, size)
             pieces.append((copy(source.at[rows], stage.at[rows]), stage.at[rows], target.at[rows]))
-    moves = []
+        if not early:
+            early = [copy(fo_in, fo), copy(sm_in, sm), copy(vx_in, vx)]
 
     def pass_on(count):
         for come, stage, target in pieces[:count]:
@@ -876,37 +927,30 @@
             moves.append(copy(stage, target))
         del pieces[:count]
 
-    for ((_, _, count, _), at), target in zip(vec_at, vec_out):
+    pass_on(SPREAD)
+    early[0].wait()
+    form, parts = forms["in"], []
+    for _, count, panels in form.plain_spans():
+        values = [fo[row : row + count, lane : lane + columns] for panel in panels for row, lane, columns in panel]
+        parts.append(jnp.concatenate(values, axis=1))
+    gi[...] = jnp.concatenate(parts, axis=0).astype(F32).T
+    moves.append(copy(gi, gi_out))
+    pass_on(SPREAD)
+    early[1].wait()
+    for tap, at in enumerate(cfg["small_at"]["conv"]):
+        gc[tap] = sm[:, at : at + width]
+    at = cfg["small_at"]["out"][0]
+    go[...] = sm[:, at : at + go.shape[1]]
+    moves += [copy(gc, gc_out), copy(go, go_out)]
+    early[2].wait()
+    for ((_, _, count, _), at), stage, target in zip(vec_at, vec_v, vec_out):
         whole = jnp.concatenate([vx[at + t : at + t + 1] for t in range(-(-count // LANES))], axis=1)
         share = count // W
         mine = jnp.zeros((1, share), F32)
         for s in range(W):
             mine = jnp.where(z == s, whole[:, s * share : (s + 1) * share], mine)
-        target[...] = mine.reshape(share)
-    grads.wait()
-    pass_on(2)
-    for name, stage, target in (("conv", gc, gc_out), ("out", go, go_out), ("in", gi, gi_out)):
-        form, base, parts = forms[name], bases[name], []
-        for start, count, panels in form.plain_spans():
-            values = [
-                [
-                    fo[base + row : base + row + count, lane : lane + columns].astype(F32)
-                    for row, lane, columns in panel
-                ]
-                for panel in panels
-            ]
-            if name == "conv":
-                for tap, part in enumerate(values):
-                    stage[tap, start : start + count] = jnp.concatenate(part, axis=1)
-            else:
-                parts.append(jnp.concatenate(sum(values, []), axis=1))
-                if name == "out":
-                    stage[start : start + count] = parts[-1]
-        if name == "in":
-            stage[...] = jnp.concatenate(parts, axis=0).T
+        stage[...] = mine.reshape(share)
         moves.append(copy(stage, target))
-        pass_on(2)
-    pass_on(len(pieces))
     for move in moves:
         move.wait()
 
@@ -944,7 +988,19 @@
         "C": C, "W": W, "J": J, "D": D, "H": H, "forms": forms, "bases": bases, "width": width, "vec_at": vec_at,
     }
     cfg["z_first"] = ("out",) if C <= 8 else ()
-    cfg["z_only"] = ("out",)
+    cfg["spans"] = {name: (bases[name], form.size) for name, form in forms.items()}
+    straight = forms["in"].size * 2 // 5
+    if C <= 8 and straight % 32 == 0 and (forms["in"].size - straight) % (16 * C) == 0:
+        cfg["in_spans"] = ("in_shared", "in_straight")
+        cfg["spans"]["in_straight"] = (bases["in"], straight)
+        cfg["spans"]["in_shared"] = (bases["in"] + straight, forms["in"].size - straight)
+    else:
+        cfg["in_spans"] = ("in",)
+    cfg["z_only"] = ("out", "in_straight")
+    cfg["small_at"] = {"conv": [tap * up(width, LANES) for tap in range(TAPS)], "out": [TAPS * up(width, LANES)]}
+    small = cfg["small_at"]["out"][0] + up(panels * width, LANES)
+    cfg["small_end"] = {"conv": cfg["small_at"]["out"][0], "out": small}
+    cfg["direct"] = ("in",) if C <= 8 else ()
     cfg["v_late"], cfg["v_rows"] = v_late, v_rows
     cfg["rz_at"], rz_rows = {}, 0
     for name in cfg["z_first"]:
@@ -953,7 +1009,7 @@
     rz_rows = max(rz_rows, 16)
     R = rows
     others = max(C // 2 - 1, 1)
-    n_groups = 3 * 3 + 2 + 2 * 2 * CHUNKS + 3 * 5 + 4
+    n_groups = 4 * 3 + 2 + 2 * 6 * CHUNKS + 3 * 5 + 4
     vmem = pltpu.VMEM
     scratch = [
         vmem((D, R), BF16),
@@ -1016,19 +1072,20 @@
     flat, tree = jax.tree.flatten(scratch)
 
     def run(*refs):
-        kernel(cfg, *refs[:20], *jax.tree.unflatten(tree, refs[20:]))
+        kernel(cfg, *refs[:21], *jax.tree.unflatten(tree, refs[21:]))
 
     macs = R * (2 * D * H + TAPS * H * H) * 3
-    bo, ig, fo, vo = pl.pallas_call(
+    bo, ig, fo, sm, vo = pl.pallas_call(
         run,
         out_shape=(
             jax.ShapeDtypeStruct((D, R), BF16),
             jax.ShapeDtypeStruct((D, R), F32),
-            jax.ShapeDtypeStruct((total, LANES), BF16),
+            jax.ShapeDtypeStruct((forms["in"].size, LANES), BF16),
+            jax.ShapeDtypeStruct((H, small), F32),
             jax.ShapeDtypeStruct((v_rows, LANES), F32),
         ),
         in_specs=[pl.BlockSpec(memory_space=pltpu.SMEM)] + [any_spec] * 15,
-        out_specs=(any_spec, any_spec, any_spec, vmem_spec),
+        out_specs=(any_spec, any_spec, any_spec, any_spec, vmem_spec),
         scratch_shapes=flat,
         compiler_params=pltpu.CompilerParams(
             collective_id=0, has_side_effects=True, vmem_limit_bytes=62 * 2**20
@@ -1057,17 +1114,18 @@
             jax.ShapeDtypeStruct((H, panels * width), F32),
         )
         + tuple(jax.ShapeDtypeStruct((item[2] // W,), F32) for item, _ in vec_at),
-        in_specs=[any_spec, any_spec, any_spec, vmem_spec],
-        out_specs=(any_spec,) * 5 + (vmem_spec,) * 9,
+        in_specs=[any_spec] * 5,
+        out_specs=(any_spec,) * 14,
         scratch_shapes=[
-            vmem((D, R), F32), vmem((D, R), BF16), vmem((total, LANES), BF16),
-            vmem((width, D), F32), vmem((TAPS, H, width), F32), vmem((H, panels * width), F32),
-            pltpu.SemaphoreType.DMA((4 * SPREAD + 4,)),
+            vmem((D, R), F32), vmem((D, R), BF16), vmem((forms["in"].size, LANES), BF16), vmem((H, small), F32),
+            vmem((v_rows, LANES), F32), vmem((width, D), F32), vmem((TAPS, H, width), F32),
+            vmem((H, panels * width), F32), *[vmem((item[2] // W,), F32) for item, _ in vec_at],
+            pltpu.SemaphoreType.DMA((4 * SPREAD + 15,)),
         ],
         compiler_params=pltpu.CompilerParams(vmem_limit_bytes=62 * 2**20),
         cost_estimate=pl.CostEstimate(flops=0, bytes_accessed=14 * R * D, transcendentals=0),
         name="spread",
-    )(bo, ig, fo, vo)
+    )(bo, ig, fo, sm, vo)
     bo, ig, gi, gc, go = results[:5]
     vec = results[5:]
     return (bo.T[None], ig.T[None], gi.T, gc, go, vec[0], vec[1], *vec[3:], vec[2])

time: 79.8 us -> 78.6 us (0.985)
  no operation moved by 1% of the time
where the time goes in v4:
time: 78.6 us; the launch traced here: 78.4 us
  Pallas kernels  77.6 us (99%)
  between operations  0.82 us (1%)
    pallas_call x1, Pallas kernels, on_device(): pl.pallas_call(run, out_shape=(jax.ShapeDtypeStruct((D, R), BF16), jax.Sh...  72.2 us
    pallas_call x1, Pallas kernels, on_device(): pl.pallas_call(lambda *refs: spread(cfg, *refs), out_shape=(jax.ShapeDtyp...  5.45 us

profile of v4, /device:TPU:0, one launch (start us, length us, event | category | flops | bytes accessed | tf_op | source)
XLA Modules:
  0.0 78.4 jit_solution(6079021985275196349)
XLA Ops:
  0.7 72.2 %block.1 = (bf16[800,1024]{1,0:T(8,128)(2,1)}, f32[800,1024]{1,0:T(8,128)}, bf16[640,128]{1,0:T(8,128)(2,1)}, f32[400,640]{1,0:T(8,128)}, f32[48,128]{1,0:T(8,128)}) custom-call(s32[64]{0:T(128)} %refs_0_.1, bf16[800,1024]{1,0:T(8,128)(2,1)} %bitcast.16, bf16[800,1024]{1,0:T(8,128)(2,1)} %bitcast.17, s32[8,128]{1,0:T(8,128)} %bitcast.21, ...), custom_call_target="tpu_custom_call" | custom-call | flops 6881280000 | bytes 8192000 | tf_op jit(solution)/shard_map/block/pallas_call | solution.py:1078
  72.8 5.5 %spread.1 = (bf16[800,1024]{1,0:T(8,128)(2,1)}, f32[800,1024]{1,0:T(8,128)}, f32[100,800]{1,0:T(8,128)}, f32[3,400,100]{2,1,0:T(8,128)}, f32[400,200]{1,0:T(8,12...) custom-call(bf16[800,1024]{1,0:T(8,128)(2,1)} %get-tuple-element.33., ...), custom_call_target="tpu_custom_call" | custom-call | bytes 11468800 | tf_op jit(solution)/shard_map/spread/pallas_call | solution.py:1107

commit v5 on v4

--- a/solution.py
+++ b/solution.py
@@ -269,6 +269,8 @@
     w_copies[0].wait()
     w_in[:, 0:width] = wi_ref[...].T
     pack("in", own_shard["in"], put_own, (0,), BF16)
+    pl.semaphore_wait(bar, C - 1 + W - 1)
+    w_z = {name: z_send(name) for name in cfg["in_spans"][:1]}
     rows = []
     for ref, copy in zip(vec_refs, vec_copies):
         copy.wait()
@@ -279,11 +281,10 @@
             )
     rows.append(jnp.zeros((16 - len(rows), LANES), F32))
     vecb[0] = jnp.concatenate(rows, axis=0).astype(BF16)
-    pl.semaphore_wait(bar, C - 1 + W - 1)
     vec_sends = copies.start(
         [(vecb.at[0], vecb.at[d + 1], planes[d]) for d in range(W - 1)], vecb.at[pl.ds(1, W - 1)]
     )
-    w_z = {name: z_send(name) for name in cfg["in_spans"]}
+    w_z.update({name: z_send(name) for name in cfg["in_spans"][1:]})
     for name, copy in (("conv", w_copies[1]), ("out", w_copies[2])):
         copy.wait()
         pack(name, own_shard[name], put_own, (0,), BF16)
@@ -341,6 +342,7 @@
         sc1[:, lanes] = lax.rsqrt(total_rows(acc) * (1.0 / D) + EPS)
 
     loop(R // LG, first_stats)
+    w_plane = {name: plane_send(name, w_z[name]) for name in cfg["in_spans"]}
 
     vec_sends.wait()
     vecs = [vecb[flip(z, s)].astype(F32) for s in shards]
@@ -368,7 +370,6 @@
             pre = normed * dup(p8[0, f], LG) + dup(p8[1, f], LG)
             a1[f, lanes] = (pre * jnp.tanh(pre) + pre).astype(BF16)
 
-    w_plane = {name: plane_send(name, w_z[name]) for name in cfg["in_spans"]}
     loop(R // LG, first_act)
     w_sib = {name: sibling_send(name, w_plane[name]) for name in cfg["in_spans"]}
     w_plane["conv"] = plane_send("conv", w_z["conv"])
@@ -501,18 +502,20 @@
     def tall(mask):
         return jnp.concatenate([mask] * (H // 16), axis=0)
 
+    t_first[0] = edge_relay(ta, t_first[0], 0)
     w_sib["conv"].wait()
     unpack("conv", w_cv)
-    t_first[0] = edge_relay(ta, t_first[0], 0)
+    t_first[1] = edge_relay(ta, t_first[1], 1)
     w_cvT[:, 0 : TAPS * H] = jnp.concatenate([w_cv[:, tap * H : (tap + 1) * H].T for tap in range(TAPS)], axis=1)
     w_sib["out"].wait()
     unpack("out", w_out)
-    t_first[1] = edge_relay(ta, t_first[1], 1)
+    t_passed.append(edge_forward(ta, t_first[0], 0))
     og_copy.wait()
     for chunk in range(CHUNKS):
         here = slice(chunk * CW, (chunk + 1) * CW)
         g3[:, here] = dot(w_out[...], og_v[:, here])
-        t_passed.append(edge_forward(ta, t_first[chunk], chunk))
+        if chunk == 0:
+            t_passed.append(edge_forward(ta, t_first[1], 1))
     edge_take(ta, t_passed, -1, pt)
 
     def third(chunk):
@@ -732,8 +735,8 @@
     pack_grad("conv")
     reduce("conv", 1)
     h_passed.append(edge_forward(ha, h_first[1], 1))
+    reduce("conv", 2)
     edge_take(ha, h_passed, 1, nh)
-    reduce("conv", 2)
 
     def second_back(chunk):
         here = slice(chunk * CW, (chunk + 1) * CW)
@@ -774,10 +777,10 @@
     second_back(0)
     second_back(1)
     big[0 : D + 16, 0:H] = dot(a1[...], gh[...], (1, 1))
-    reduce("out", 3)
-    keep_row(7, big[D : D + 1, 0:H])
     pack_grad("in")
     reduce("in", 1)
+    keep_row(7, big[D : D + 1, 0:H])
+    reduce("out", 3)
 
     def sums_rows(indices):
         for index in indices:
@@ -807,7 +810,6 @@
     late, early = slice(0, cfg["v_late"]), slice(cfg["v_late"], cfg["v_rows"])
     sums_rows((3, 4, 5, 6))
     v_early = sums_plane(early)
-    reduce("conv", 3)
     for side in range(D // H):
         w_cvT[:, side * 512 : side * 512 + H] = w_out[:, side * H : (side + 1) * H].T
 
@@ -874,11 +876,12 @@
 
     out_copies = [first_back(0)]
     reduce("in", 2)
+    reduce("conv", 3)
     out_copies.append(first_back(1))
     sums_rows((0, 1))
     v_late = sums_plane(late)
+    reduce("in", 3)
     v_early = sums_column(early, v_early)
-    reduce("in", 3)
     reduce("conv", 4)
     out_copies.append(last(0))
     v_late = sums_column(late, v_late)

time: 78.6 us -> 77.3 us (0.983)
  Pallas kernels: 77.6 us -> 76.3 us
    pallas_call x1, Pallas kernels: 72.2 us -> 70.9 us  [on_device(): pl.pallas_call(run, out_shape=(jax.ShapeDtypeStruct((D, R), BF16), jax.Sh...]
where the time goes in v5:
time: 77.3 us; the launch traced here: 77.2 us
  Pallas kernels  76.3 us (99%)
  between operations  0.82 us (1%)
    pallas_call x1, Pallas kernels, on_device(): pl.pallas_call(run, out_shape=(jax.ShapeDtypeStruct((D, R), BF16), jax.Sh...  70.9 us
    pallas_call x1, Pallas kernels, on_device(): pl.pallas_call(lambda *refs: spread(cfg, *refs), out_shape=(jax.ShapeDtyp...  5.45 us

profile of v5, /device:TPU:0, one launch (start us, length us, event | category | flops | bytes accessed | tf_op | source)
XLA Modules:
  0.0 77.2 jit_solution(6018416528050590063)
XLA Ops:
  0.7 70.9 %block.1 = (bf16[800,1024]{1,0:T(8,128)(2,1)}, f32[800,1024]{1,0:T(8,128)}, bf16[640,128]{1,0:T(8,128)(2,1)}, f32[400,640]{1,0:T(8,128)}, f32[48,128]{1,0:T(8,128)}) custom-call(s32[64]{0:T(128)} %refs_0_.1, bf16[800,1024]{1,0:T(8,128)(2,1)} %bitcast.16, bf16[800,1024]{1,0:T(8,128)(2,1)} %bitcast.17, s32[8,128]{1,0:T(8,128)} %bitcast.21, ...), custom_call_target="tpu_custom_call" | custom-call | flops 6881280000 | bytes 8192000 | tf_op jit(solution)/shard_map/block/pallas_call | solution.py:1081
  71.6 5.5 %spread.1 = (bf16[800,1024]{1,0:T(8,128)(2,1)}, f32[800,1024]{1,0:T(8,128)}, f32[100,800]{1,0:T(8,128)}, f32[3,400,100]{2,1,0:T(8,128)}, f32[400,200]{1,0:T(8,12...) custom-call(bf16[800,1024]{1,0:T(8,128)(2,1)} %get-tuple-element.33., ...), custom_call_target="tpu_custom_call" | custom-call | bytes 11468800 | tf_op jit(solution)/shard_map/spread/pallas_call | solution.py:1110
